TPU v7x, 1024 devices: a whole 8x8x8 slice. The times are simulated.
1024 devices in a mesh: replica: 32 (over z_lo, y, core), mp: 32 (over x, z_hi).
Axes of the slice: x: 8, y: 8, z: 8 (z_hi: 4, z_lo: 2; z = z_hi * 2 + z_lo), core: 2. Of those that a mesh axis runs over, the one named last changes fastest.
Arguments:
- code_table: int32 [16], replicated, may hold values from -7 to 7
- up_codes: int32 [32, 2, 32, 28672], P('replica', None, None, 'mp'), may hold values from 0 to 15
- up_exps: int32 [32, 2, 32, 224], P('replica', None, None, 'mp'), may hold values from -8 to -3
- up_global: float32 [2, 32, 28672], P(None, 'replica', 'mp'), may hold values from -6 to 6
- up_moment: float32 [2, 32, 28672], P(None, 'replica', 'mp'), may hold values from -4 to 4
- up_local: bfloat16 [32, 2, 32, 28672], P('replica', None, None, 'mp'), may hold values from -6 to 6
- down_codes: int32 [32, 32, 8192], P('replica', None, 'mp'), may hold values from 0 to 15
- down_exps: int32 [32, 32, 64], P('replica', None, 'mp'), may hold values from -8 to -3
- down_global: float32 [32, 8192], P('replica', 'mp'), may hold values from -6 to 6
- down_moment: float32 [32, 8192], P('replica', 'mp'), may hold values from -4 to 4
- down_local: bfloat16 [32, 32, 8192], P('replica', None, 'mp'), may hold values from -6 to 6
Outputs:
- up_global_new: float32 [2, 32, 28672], P(None, 'replica', 'mp')
- up_moment_new: float32 [2, 32, 28672], P(None, 'replica', 'mp')
- up_merged: bfloat16 [32, 2, 32, 28672], P('replica', None, None, 'mp')
- down_global_new: float32 [32, 8192], P('replica', 'mp')
- down_moment_new: float32 [32, 8192], P('replica', 'mp')
- down_merged: bfloat16 [32, 32, 8192], P('replica', None, 'mp')
All inputs are finite; a program needn't handle non-finite values.
Results may differ from a plain program's by a relative error of at most 0.0044.
Values may be sent and summed in bfloat16 or wider, within the bound.
No kernel may reach another device: no remote copies, remote signals or barrier semaphores. Data moves between devices by JAX's collectives and lax.ppermute only.
A program may use at most 32 MiB of HBM per device.

v0:
```python
import jax
import jax.numpy as jnp
from jax import lax
from jax.sharding import PartitionSpec as P

BLOCK = 128


outer_rate = 0.7
nesterov = 0.9
mixing = 0.5


def decode(codes, exps, code_table):
    table = code_table.astype(jnp.float32)
    values = jnp.zeros(codes.shape, jnp.float32)
    for level in range(16):
        values = values + jnp.where(codes == level, table[level], 0.0)
    shape = codes.shape
    blocks = shape[-1] // BLOCK
    values = values.reshape(shape[:-1] + (blocks, BLOCK))
    scales = jnp.exp2(exps.astype(jnp.float32))[..., None]
    return (values * scales).reshape(shape).astype(jnp.bfloat16)


def advance(received, weights, moment):
    total = jnp.sum(received.astype(jnp.float32), axis=0)
    mean = total / received.shape[0]
    moment_new = nesterov * moment + mean
    weights_new = weights - outer_rate * (mean + nesterov * moment_new)
    return (weights_new, moment_new)


def per_device(
    code_table,
    up_codes,
    up_exps,
    up_global,
    up_moment,
    up_local,
    down_codes,
    down_exps,
    down_global,
    down_moment,
    down_local,
):
    up_plain = decode(up_codes, up_exps, code_table)
    up_recv = lax.all_to_all(up_plain, "replica", split_axis=2, concat_axis=0, tiled=True)
    down_plain = decode(down_codes, down_exps, code_table)
    down_recv = lax.all_to_all(down_plain, "replica", split_axis=1, concat_axis=0, tiled=True)
    up_new, up_mom = advance(up_recv, up_global, up_moment)
    down_new, down_mom = advance(down_recv, down_global, down_moment)
    mine = up_local
    up_merged = (
        mixing * mine.astype(jnp.float32)
        + (1.0 - mixing)
        * lax.all_gather(up_new.astype(jnp.bfloat16), "replica", axis=1, tiled=True).astype(
            jnp.float32
        )[None]
    ).astype(jnp.bfloat16)
    mine = down_local
    down_merged = (
        mixing * mine.astype(jnp.float32)
        + (1.0 - mixing)
        * lax.all_gather(down_new.astype(jnp.bfloat16), "replica", axis=0, tiled=True).astype(
            jnp.float32
        )[None]
    ).astype(jnp.bfloat16)
    return (up_new, up_mom, up_merged, down_new, down_mom, down_merged)


def solution(mesh):
    in_specs = (
        P(),
        P("replica", None, None, "mp"),
        P("replica", None, None, "mp"),
        P(None, "replica", "mp"),
        P(None, "replica", "mp"),
        P("replica", None, None, "mp"),
        P("replica", None, "mp"),
        P("replica", None, "mp"),
        P("replica", "mp"),
        P("replica", "mp"),
        P("replica", None, "mp"),
    )
    out_specs = (
        P(None, "replica", "mp"),
        P(None, "replica", "mp"),
        P("replica", None, None, "mp"),
        P("replica", "mp"),
        P("replica", "mp"),
        P("replica", None, "mp"),
    )
    return jax.shard_map(
        per_device, mesh=mesh, in_specs=in_specs, out_specs=out_specs, check_vma=False
    )
```

profile of v0, /device:TPU:1, one launch (start us, length us, event | category | flops | bytes accessed | tf_op | source)
XLA Modules:
  0.0 123.9 jit_solution(4331208332654749720)
XLA Ops:
  0.6 0.7 convert_element_type.66
  1.3 0.0 copy-start.7
  1.3 0.7 fusion.8
  2.0 0.0 copy-done.7
  2.0 0.1 copy.69
  2.1 0.1 mul.74
  2.2 0.0 copy-start.2
  2.3 0.7 copy-done.2
  3.0 10.2 %multiply_convert_fusion.1 = bf16[1,32,256]{2,1,0:T(8,128)(2,1)S(1)} fusion(f32[1,32,256]{2,1,0:T(8,128)S(1)} %mul.75, s32[1,32,256]{2,1,0:T(8,128)S(1)} %copy-done.2, f32[]{:T(128)} %bitcast.15, f32[]{:T(128)} %bitcast.14, f32[]{:T(128)} %bitcast.13, f32[]{:T(128)} %bitcast.12, f32[]{:T(128)} %bitcast.11, f32[]{:T(128)} %bitcast.10, f32[]{:T(128)} %bitcast.9, ...), kind=kLoop, calls=%fused_computation.10 | loop fusion | flops 401408 | bytes 81984 | tf_op jit(solution)/shard_map/convert_element_type | solution.py:23
  13.2 0.5 broadcast.57
  13.7 0.7 reduce.6
  14.5 0.6 reshape.96
  15.1 0.0 copy-start.6
  15.1 17.8 %all-to-all-start.1 = ((bf16[32,2,128]{2,1,0:T(2,128)(2,1)}), bf16[32,2,128]{2,1,0:T(2,128)(2,1)S(1)}, u32[]{:S(2)}, u32[]{:S(2)}) async-start(bf16[32,2,128]{2,1,0:T(2,128)(2,1)} %reshape.96), calls=%async_computation.1 | async-start | bytes 32768 | tf_op jit(solution)/shard_map/all_to_all | solution.py:50
  32.9 0.0 copy-done.6
  32.9 0.1 copy.64
  33.0 0.1 mul.65
  33.1 0.0 copy-start
  33.2 0.9 copy-done
  34.1 10.5 %multiply_convert_fusion = bf16[1,2,32,896]{3,2,1,0:T(8,128)(2,1)S(1)} fusion(f32[1,2,32,896]{3,2,1,0:T(8,128)S(1)} %mul.66, s32[1,2,32,896]{3,2,1,0:T(8,128)S(1)} %copy-done, f32[]{:T(128)} %bitcast.15, f32[]{:T(128)} %bitcast.14, f32[]{:T(128)} %bitcast.13, f32[]{:T(128)} %bitcast.12, f32[]{:T(128)} %bitcast.11, f32[]{:T(128)} %bitcast.10, f32[]{:T(128)} %bitcast.9, ...), kind=kLoop, calls=%fused_computation.4 | loop fusion | flops 2809856 | bytes 573504 | tf_op jit(solution)/shard_map/convert_element_type | solution.py:23
  44.5 0.7 copy.65
  45.3 0.0 all-to-all-done.1
  45.3 8.4 %all-to-all-start = ((bf16[1,2,32,896]{3,1,0,2:T(2,128)(2,1)}), bf16[1,2,32,896]{3,1,0,2:T(2,128)(2,1)S(1)}, u32[]{:S(2)}, u32[]{:S(2)}) async-start(bf16[1,2,32,896]{3,1,0,2:T(2,128)(2,1)} %copy.65), calls=%async_computation | async-start | bytes 229376 | tf_op jit(solution)/shard_map/all_to_all | solution.py:48
  53.7 0.0 copy-start.9
  53.7 0.1 convert_reduce_fusion.1
  53.8 0.0 copy-start.8
  53.8 0.6 copy-done.9
  54.4 0.1 copy-done.8
  54.5 0.6 convert_bitcast_fusion
  55.0 0.0 copy-start.3
  55.0 34.5 %all-gather = bf16[32,1,256]{2,1,0:T(2,128)(2,1)S(1)} all-gather(bf16[1,1,256]{2,1,0:T(2,128)(2,1)S(1)} %get-tuple-element.18), channel_id=1, replica_groups=mesh['replica'=32,'mp'=32] {'replica'}, dimensions={0}, use_global_device_ids=true | all-gather | bytes 16896 | tf_op jit(solution)/shard_map/all_gather | solution.py:65
  89.6 0.0 copy-done.3
  89.6 0.6 copy.75
  90.2 0.0 copy-start.4
  90.2 0.0 copy-start.5
  90.2 0.0 all-to-all-done
  90.2 0.1 convert_reduce_fusion
  90.3 0.6 copy-done.4
  90.9 0.0 copy-done.5
  90.9 0.0 copy-start.1
  91.0 0.6 copy.72
  91.6 0.6 copy.73
  92.2 31.0 %all_gather.6 = bf16[2,32,896]{2,0,1:T(2,128)(2,1)S(1)} all-gather(bf16[2,1,896]{2,0,1:T(2,128)(2,1)S(1)} %get-tuple-element.21), channel_id=1, replica_groups=mesh['replica'=32,'mp'=32] {'replica'}, dimensions={1}, use_global_device_ids=true | all-gather | bytes 118272 | tf_op jit(solution)/shard_map/all_gather | solution.py:57
  123.1 0.0 copy-done.1
  123.1 0.1 fusion.1
  123.3 0.7 copy.74
  (9 shorter events, 0.2 us)
Async XLA Ops:
  1.3 0.7 copy-start.7
  2.2 0.8 copy-start.2
  15.1 17.8 %copy-start.6 = (s32[1,2,32,7]{2,1,3,0:T(2,128)S(1)}, s32[1,2,32,7]{2,1,3,0:T(2,128)}, u32[]{:S(2)}) copy-start(s32[1,2,32,7]{2,1,3,0:T(2,128)} %param.13) | copy-start | bytes 5380
  15.1 30.2 %all-to-all-start.1 = ((bf16[32,2,128]{2,1,0:T(2,128)(2,1)}), bf16[32,2,128]{2,1,0:T(2,128)(2,1)S(1)}, u32[]{:S(2)}, u32[]{:S(2)}) async-start(bf16[32,2,128]{2,1,0:T(2,128)(2,1)} %reshape.96), calls=%async_computation.1 | async-start | bytes 32768 | tf_op jit(solution)/shard_map/all_to_all | solution.py:50
  33.1 0.9 copy-start
  45.3 45.0 %all-to-all-start = ((bf16[1,2,32,896]{3,1,0,2:T(2,128)(2,1)}), bf16[1,2,32,896]{3,1,0,2:T(2,128)(2,1)S(1)}, u32[]{:S(2)}, u32[]{:S(2)}) async-start(bf16[1,2,32,896]{3,1,0,2:T(2,128)(2,1)} %copy.65), calls=%async_computation | async-start | bytes 229376 | tf_op jit(solution)/shard_map/all_to_all | solution.py:48
  53.7 0.7 copy-start.9
  53.8 0.7 copy-start.8
  55.0 34.5 %copy-start.3 = (bf16[1,32,256]{2,1,0:T(8,128)(2,1)S(1)}, bf16[1,32,256]{2,1,0:T(8,128)(2,1)}, u32[]{:S(2)}) copy-start(bf16[1,32,256]{2,1,0:T(8,128)(2,1)} %param.21) | copy-start | bytes 49156
  90.2 0.7 copy-start.4
  90.2 0.7 copy-start.5
  90.9 32.2 %copy-start.1 = (bf16[1,2,32,896]{3,2,1,0:T(8,128)(2,1)S(1)}, bf16[1,2,32,896]{3,2,1,0:T(8,128)(2,1)}, u32[]{:S(2)}) copy-start(bf16[1,2,32,896]{3,2,1,0:T(8,128)(2,1)} %param.16) | copy-start | bytes 344068
where the time goes:
time: 125 us; the launch traced here: 124 us
  blocking collectives  65.5 us (52%)
  starting transfers between devices  26.2 us (21%)
  other arithmetic  23 us (18%)
  local copies, waits for them, and re-layouts  8.5 us (7%)
    all_gather x1, blocking collectives, per_device(): lax.all_gather(down_new.astype(jnp.bfloat16), 'replica', axis=0, tiled=True)  34.5 us
    all_gather x1, blocking collectives, per_device(): lax.all_gather(up_new.astype(jnp.bfloat16), 'replica', axis=1, tiled=True)  31 us
    convert_element_type x2, other arithmetic, decode(): return (values * scales).reshape(shape).astype(jnp.bfloat16)  20.6 us
    all_to_all x1, starting transfers between devices, per_device(): lax.all_to_all(down_plain, 'replica', split_axis=1, concat_axis=0, tiled=...  17.8 us
    all_to_all x1, starting transfers between devices, per_device(): lax.all_to_all(up_plain, 'replica', split_axis=2, concat_axis=0, tiled=True)  8.42 us
    unnamed x27, local copies, waits for them, and re-layouts  6.54 us
  transfers between devices with their start and end apart: 2, of which 0 were waited for; matrix products, arithmetic and copies ran while one was open for 10% of the time, Pallas kernels for 0%

commit v1 on v0

v1 whole, which is shorter than its diff:
```python
import jax
import jax.numpy as jnp
from jax import lax
from jax.experimental import pallas as pl
from jax.experimental.pallas import tpu as pltpu
from jax.sharding import PartitionSpec as P

LANES = 128
LOW_EXP = -8

outer_rate = 0.7
nesterov = 0.9
mixing = 0.5

VMEM = pl.BlockSpec(memory_space=pltpu.VMEM)
SMEM = pl.BlockSpec(memory_space=pltpu.SMEM)


def up_slots(groups, blocks):
    return [(s * groups + g, g, s) for s in range(blocks) for g in range(groups)]


def decode_kernel(table_ref, up_codes, up_exps, down_codes, down_exps, out_ref, codes_by_row, exps_by_slot):
    groups, rows, width = up_codes.shape
    up_blocks = width // LANES
    down_blocks = down_codes.shape[1] // LANES
    slots = groups * up_blocks + down_blocks
    for j, g, s in up_slots(groups, up_blocks):
        codes_by_row[pl.ds(j, rows, stride=slots), :] = up_codes[g, :, s * LANES : (s + 1) * LANES]
        exps_by_slot[j : j + 1, :] = up_exps[s, g : g + 1, :]
    for t in range(down_blocks):
        j = groups * up_blocks + t
        codes_by_row[pl.ds(j, rows, stride=slots), :] = down_codes[:, t * LANES : (t + 1) * LANES]
        exps_by_slot[j : j + 1, :] = down_exps[t : t + 1, :]
    lane = lax.broadcasted_iota(jnp.int32, (slots, LANES), 1)
    table = jnp.zeros((slots, LANES), jnp.int32)
    for level in range(16):
        table = jnp.where(lane == level, table_ref[level], table)
    scales = jnp.left_shift(1, exps_by_slot[...] - LOW_EXP).astype(jnp.float32) * 2.0**LOW_EXP
    table = table.astype(jnp.float32)
    for r in range(rows):
        codes = codes_by_row[r * slots : (r + 1) * slots, :]
        values = jnp.take_along_axis(table, codes, axis=1)
        out_ref[r] = (values * scales[:, r : r + 1]).astype(jnp.bfloat16)


def advance_kernel(
    recv, up_global, up_moment, down_global, down_moment,
    up_new, up_mom, down_new, down_mom, out_ref, weights, moment,
):
    groups, _, width = up_global.shape
    up_blocks = width // LANES
    down_blocks = down_global.shape[1] // LANES
    places = [
        (j, (g, slice(0, 1), slice(s * LANES, (s + 1) * LANES))) for j, g, s in up_slots(groups, up_blocks)
    ]
    down_places = [
        (groups * up_blocks + t, (slice(0, 1), slice(t * LANES, (t + 1) * LANES))) for t in range(down_blocks)
    ]
    for j, at in places:
        weights[j : j + 1, :] = up_global[at]
        moment[j : j + 1, :] = up_moment[at]
    for j, at in down_places:
        weights[j : j + 1, :] = down_global[at]
        moment[j : j + 1, :] = down_moment[at]
    total = jnp.sum(recv[...].astype(jnp.float32), axis=0)
    mean = total / recv.shape[0]
    moment_new = nesterov * moment[...] + mean
    weights_new = weights[...] - outer_rate * (mean + nesterov * moment_new)
    shared = weights_new.astype(jnp.bfloat16)
    for r in range(out_ref.shape[0]):
        out_ref[r] = shared
    weights[...] = weights_new
    moment[...] = moment_new
    for j, at in places:
        up_new[at] = weights[j : j + 1, :]
        up_mom[at] = moment[j : j + 1, :]
    for j, at in down_places:
        down_new[at] = weights[j : j + 1, :]
        down_mom[at] = moment[j : j + 1, :]


def merge_kernel(recv, up_local, down_local, up_merged, down_merged, shared):
    groups, rows, width = up_local.shape
    up_blocks = width // LANES
    down_blocks = down_local.shape[1] // LANES
    slots = recv.shape[1]
    for r in range(rows):
        shared[r * slots : (r + 1) * slots, :] = recv[r].astype(jnp.float32)

    def merged(local, j):
        theirs = shared[pl.ds(j, rows, stride=slots), :]
        return (mixing * local.astype(jnp.float32) + (1.0 - mixing) * theirs).astype(jnp.bfloat16)

    for j, g, s in up_slots(groups, up_blocks):
        at = (g, slice(None), slice(s * LANES, (s + 1) * LANES))
        up_merged[at] = merged(up_local[at], j)
    for t in range(down_blocks):
        at = (slice(None), slice(t * LANES, (t + 1) * LANES))
        down_merged[at] = merged(down_local[at], groups * up_blocks + t)


def per_device(
    code_table,
    up_codes,
    up_exps,
    up_global,
    up_moment,
    up_local,
    down_codes,
    down_exps,
    down_global,
    down_moment,
    down_local,
):
    _, groups, rows, width = up_codes.shape
    depth = down_codes.shape[-1]
    slots = (groups * width + depth) // LANES
    chunk = jax.ShapeDtypeStruct((rows, slots, LANES), jnp.bfloat16)
    sds = jax.ShapeDtypeStruct
    decoded = pl.pallas_call(
        decode_kernel,
        out_shape=chunk,
        in_specs=[SMEM, VMEM, VMEM, VMEM, VMEM],
        out_specs=VMEM,
        scratch_shapes=[pltpu.VMEM((rows * slots, LANES), jnp.int32), pltpu.VMEM((slots, rows), jnp.int32)],
    )(
        code_table,
        up_codes[0],
        jnp.transpose(up_exps[0], (2, 0, 1)),
        down_codes[0],
        jnp.transpose(down_exps[0], (1, 0)),
    )
    recv = lax.all_to_all(decoded, "replica", split_axis=0, concat_axis=0, tiled=True)
    up_new, up_mom, down_new, down_mom, shared = pl.pallas_call(
        advance_kernel,
        out_shape=(
            sds(up_global.shape, jnp.float32),
            sds(up_global.shape, jnp.float32),
            sds(down_global.shape, jnp.float32),
            sds(down_global.shape, jnp.float32),
            chunk,
        ),
        in_specs=[VMEM] * 5,
        out_specs=(VMEM,) * 5,
        scratch_shapes=[pltpu.VMEM((slots, LANES), jnp.float32), pltpu.VMEM((slots, LANES), jnp.float32)],
    )(recv, up_global, up_moment, down_global, down_moment)
    spread = lax.all_to_all(shared, "replica", split_axis=0, concat_axis=0, tiled=True)
    up_merged, down_merged = pl.pallas_call(
        merge_kernel,
        out_shape=(sds(up_local.shape[1:], jnp.bfloat16), sds(down_local.shape[1:], jnp.bfloat16)),
        in_specs=[VMEM] * 3,
        out_specs=(VMEM,) * 2,
        scratch_shapes=[pltpu.VMEM((rows * slots, LANES), jnp.float32)],
    )(spread, up_local[0], down_local[0])
    return (up_new, up_mom, up_merged[None], down_new, down_mom, down_merged[None])


def solution(mesh):
    in_specs = (
        P(),
        P("replica", None, None, "mp"),
        P("replica", None, None, "mp"),
        P(None, "replica", "mp"),
        P(None, "replica", "mp"),
        P("replica", None, None, "mp"),
        P("replica", None, "mp"),
        P("replica", None, "mp"),
        P("replica", "mp"),
        P("replica", "mp"),
        P("replica", None, "mp"),
    )
    out_specs = (
        P(None, "replica", "mp"),
        P(None, "replica", "mp"),
        P("replica", None, None, "mp"),
        P("replica", "mp"),
        P("replica", "mp"),
        P("replica", None, "mp"),
    )
    return jax.shard_map(
        per_device, mesh=mesh, in_specs=in_specs, out_specs=out_specs, check_vma=False
    )
```

time: 125 us -> 48.8 us (0.39)
  starting transfers between devices: 26.2 us -> 0 us
  other arithmetic: 23 us -> 0 us
  blocking collectives: 65.5 us -> 42.5 us
  local copies, waits for them, and re-layouts: 8.5 us -> 0 us
  Pallas kernels: 0 us -> 5.39 us
    all_gather x2 -> x0, blocking collectives: 65.5 us -> none  [the longest x1 34.5 us: per_device(): lax.all_gather(down_new.astype(jnp.bfloat16), 'replica', axis=0, tiled=True)]
    all_to_all x0 -> x2, blocking collectives: none -> 42.5 us  [the longest x1 27.5 us: per_device(): lax.all_to_all(decoded, 'replica', split_axis=0, concat_axis=0, tiled=True)]
    all_to_all x2 -> x0, starting transfers between devices: 26.2 us -> none  [the longest x1 17.8 us: per_device(): lax.all_to_all(down_plain, 'replica', split_axis=1, concat_axis=0, tiled=...]
    convert_element_type x6 -> x0, other arithmetic: 21.5 us -> none  [the longest x2 20.6 us: decode(): return (values * scales).reshape(shape).astype(jnp.bfloat16)]
    unnamed x27 -> x0, local copies, waits for them, and re-layouts: 6.54 us -> none
    pallas_call x0 -> x3, Pallas kernels: none -> 5.39 us  [the longest x1 2.01 us: per_device(): pl.pallas_call(decode_kernel, out_shape=chunk, in_specs=[SMEM, VMEM, VMEM...]
    unnamed x2 -> x0, other arithmetic: 1.3 us -> none
  transfers between devices with their start and end apart: 2 -> 0, of which waited for: 0 -> 0; matrix products, arithmetic and copies ran while one was open for 10% -> 0% of each run, Pallas kernels for 0% -> 0%
where the time goes in v1:
time: 48.8 us; the launch traced here: 48.5 us
  blocking collectives  42.5 us (87%)
  Pallas kernels  5.39 us (11%)
  between operations  0.64 us (1%)
    all_to_all x1, blocking collectives, per_device(): lax.all_to_all(decoded, 'replica', split_axis=0, concat_axis=0, tiled=True)  27.5 us
    all_to_all x1, blocking collectives, per_device(): lax.all_to_all(shared, 'replica', split_axis=0, concat_axis=0, tiled=True)  15 us
    pallas_call x1, Pallas kernels, per_device(): pl.pallas_call(decode_kernel, out_shape=chunk, in_specs=[SMEM, VMEM, VMEM...  2.01 us
    pallas_call x1, Pallas kernels, per_device(): pl.pallas_call(merge_kernel, out_shape=(sds(up_local.shape[1:], jnp.bfloa...  1.72 us
    pallas_call x1, Pallas kernels, per_device(): pl.pallas_call(advance_kernel, out_shape=(sds(up_global.shape, jnp.float3...  1.66 us

profile of v1, /device:TPU:1, one launch (start us, length us, event | category | flops | bytes accessed | tf_op | source)
XLA Modules:
  0.0 48.5 jit_solution(8804909153439759344)
XLA Ops:
  0.6 2.0 %shard_map.154 = bf16[32,16,128]{2,1,0:T(8,128)(2,1)} custom-call(s32[16]{0:T(128)} %table_ref.1, s32[2,32,896]{2,1,0:T(8,128)} %bitcast.12, s32[7,2,32]{2,1,0:T(2,128)} %bitcast.16, s32[32,256]{1,0:T(8,128)} %bitcast.14, s32[2,32]{1,0:T(2,128)} %bitcast.17), custom_call_target="tpu_custom_call" | custom-call | tf_op jit(solution)/shard_map/pallas_call | solution.py:121
  2.6 27.5 %all_to_all.10.recv = bf16[32,16,128]{2,1,0:T(8,128)(2,1)} all-to-all(bf16[32,16,128]{2,1,0:T(8,128)(2,1)} %shard_map.154), channel_id=1, replica_groups=mesh['replica'=32,'mp'=32] {'replica'}, dimensions={0} | all-to-all | bytes 262144 | tf_op jit(solution)/shard_map/all_to_all | solution.py:134
  30.1 1.7 %shard_map.155 = (f32[2,1,896]{2,1,0:T(1,128)}, f32[2,1,896]{2,1,0:T(1,128)}, f32[1,256]{1,0:T(1,128)}, f32[1,256]{1,0:T(1,128)}, bf16[32,16,128]{2,1,0:T(8,128)(2,1)}) custom-call(bf16[32,16,128]{2,1,0:T(8,128)(2,1)} %all_to_all.10.recv, f32[2,1,896]{2,1,0:T(1,128)} %up_global.1, f32[2,1,896]{2,1,0:T(1,128)} %up_moment.1, f32[1,256]{1,0:T(1,128)} %down_global.1, ...), custom_call_target="tpu_custom_call" | custom-call | tf_op jit(solution)/shard_map/pallas_call | solution.py:135
  31.8 15.0 %all_to_all.11.recv = bf16[32,16,128]{2,1,0:T(8,128)(2,1)} all-to-all(bf16[32,16,128]{2,1,0:T(8,128)(2,1)} %get-tuple-element.15), channel_id=1, replica_groups=mesh['replica'=32,'mp'=32] {'replica'}, dimensions={0} | all-to-all | bytes 262144 | tf_op jit(solution)/shard_map/all_to_all | solution.py:148
  46.8 1.7 %shard_map.156 = (bf16[2,32,896]{2,1,0:T(8,128)(2,1)}, bf16[32,256]{1,0:T(8,128)(2,1)}) custom-call(bf16[32,16,128]{2,1,0:T(8,128)(2,1)} %all_to_all.11.recv, bf16[2,32,896]{2,1,0:T(8,128)(2,1)} %bitcast.13, bf16[32,256]{1,0:T(8,128)(2,1)} %bitcast.15), custom_call_target="tpu_custom_call" | custom-call | tf_op jit(solution)/shard_map/pallas_call | solution.py:149

commit v2 on v1

v2 whole, which is shorter than its diff:
```python
import jax
import jax.numpy as jnp
from jax import lax
from jax.experimental import pallas as pl
from jax.experimental.pallas import tpu as pltpu
from jax.sharding import PartitionSpec as P

LANES = 128
LOW_EXP = -8

outer_rate = 0.7
nesterov = 0.9
mixing = 0.5

VMEM = pl.BlockSpec(memory_space=pltpu.VMEM)
HBM = pl.BlockSpec(memory_space=pltpu.HBM)


PARAMS = pltpu.CompilerParams(vmem_limit_bytes=4 * 1024 * 1024)


def up_slots(groups, blocks):
    return [(s * groups + g, g, s) for s in range(blocks) for g in range(groups)]


def decode_kernel(
    table_hbm, up_codes_hbm, up_exps_hbm, down_codes_hbm, down_exps_hbm, out_ref,
    table_ref, up_codes, up_exps, down_codes, down_exps, codes_by_row, exps_by_slot, sems,
):
    copies = [
        pltpu.make_async_copy(source, target, sems.at[i])
        for i, (source, target) in enumerate(
            [
                (table_hbm, table_ref),
                (up_exps_hbm, up_exps),
                (down_exps_hbm, down_exps),
                (down_codes_hbm, down_codes),
                (up_codes_hbm, up_codes),
            ]
        )
    ]
    for copy in copies:
        copy.start()
    groups, rows, width = up_codes.shape
    up_blocks = width // LANES
    down_blocks = down_codes.shape[1] // LANES
    slots = groups * up_blocks + down_blocks
    copies[0].wait()
    lane = lax.broadcasted_iota(jnp.int32, (slots, LANES), 1)
    table = jnp.zeros((slots, LANES), jnp.int32)
    for level in range(16):
        table = jnp.where(lane == level, table_ref[level], table)
    table = table.astype(jnp.float32)
    for copy in copies[1:4]:
        copy.wait()
    for j, g, s in up_slots(groups, up_blocks):
        exps_by_slot[j : j + 1, :] = up_exps[s, g : g + 1, :]
    for t in range(down_blocks):
        j = groups * up_blocks + t
        codes_by_row[pl.ds(j, rows, stride=slots), :] = down_codes[:, t * LANES : (t + 1) * LANES]
        exps_by_slot[j : j + 1, :] = down_exps[t : t + 1, :]
    scales = jnp.left_shift(1, exps_by_slot[...] - LOW_EXP).astype(jnp.float32) * 2.0**LOW_EXP
    copies[4].wait()
    for j, g, s in up_slots(groups, up_blocks):
        codes_by_row[pl.ds(j, rows, stride=slots), :] = up_codes[g, :, s * LANES : (s + 1) * LANES]
    for r in range(rows):
        codes = codes_by_row[r * slots : (r + 1) * slots, :]
        values = jnp.take_along_axis(table, codes, axis=1)
        out_ref[r] = (values * scales[:, r : r + 1]).astype(jnp.bfloat16)


def chip_sum_kernel(recv, up_global, up_moment, down_global, down_moment, out_ref):
    groups, _, width = up_global.shape
    up_blocks = width // LANES
    for k in range(2):
        total = recv[k].astype(jnp.float32)
        for q in range(1, recv.shape[0] // 2):
            total = total + recv[2 * q + k].astype(jnp.float32)
        out_ref[k] = total
    for j, g, s in up_slots(groups, up_blocks):
        out_ref[2, j : j + 1, :] = up_global[g, :, s * LANES : (s + 1) * LANES]
        out_ref[3, j : j + 1, :] = up_moment[g, :, s * LANES : (s + 1) * LANES]
    for t in range(down_global.shape[1] // LANES):
        j = groups * up_blocks + t
        out_ref[2, j : j + 1, :] = down_global[:, t * LANES : (t + 1) * LANES]
        out_ref[3, j : j + 1, :] = down_moment[:, t * LANES : (t + 1) * LANES]


def advance_kernel(both, up_new, up_mom, down_new, down_mom, out_ref, weights, moment):
    core = lax.rem(lax.axis_index("replica"), 2)
    replicas = out_ref.shape[0]
    for k in range(2):
        mean = (both[k] + both[4 + k]) / replicas
        moment_new = nesterov * both[4 * k + 3] + mean
        weights_new = both[4 * k + 2] - outer_rate * (mean + nesterov * moment_new)
        shared = weights_new.astype(jnp.bfloat16)
        for q in range(replicas // 2):
            out_ref[2 * q + k] = shared
        weights[k] = weights_new
        moment[k] = moment_new
    groups, _, width = up_new.shape
    up_blocks = width // LANES
    for j, g, s in up_slots(groups, up_blocks):
        up_new[g, :, s * LANES : (s + 1) * LANES] = weights[core, j : j + 1, :]
        up_mom[g, :, s * LANES : (s + 1) * LANES] = moment[core, j : j + 1, :]
    for t in range(down_new.shape[1] // LANES):
        j = groups * up_blocks + t
        down_new[:, t * LANES : (t + 1) * LANES] = weights[core, j : j + 1, :]
        down_mom[:, t * LANES : (t + 1) * LANES] = moment[core, j : j + 1, :]


def merge_kernel(recv, up_local, down_local, up_merged, down_merged, shared):
    groups, rows, width = up_local.shape
    up_blocks = width // LANES
    down_blocks = down_local.shape[1] // LANES
    slots = recv.shape[1]
    for r in range(rows):
        shared[r * slots : (r + 1) * slots, :] = recv[r].astype(jnp.float32)

    def merged(local, j):
        theirs = shared[pl.ds(j, rows, stride=slots), :]
        return (mixing * local.astype(jnp.float32) + (1.0 - mixing) * theirs).astype(jnp.bfloat16)

    for j, g, s in up_slots(groups, up_blocks):
        at = (g, slice(None), slice(s * LANES, (s + 1) * LANES))
        up_merged[at] = merged(up_local[at], j)
    for t in range(down_blocks):
        at = (slice(None), slice(t * LANES, (t + 1) * LANES))
        down_merged[at] = merged(down_local[at], groups * up_blocks + t)


def per_device(
    code_table,
    up_codes,
    up_exps,
    up_global,
    up_moment,
    up_local,
    down_codes,
    down_exps,
    down_global,
    down_moment,
    down_local,
):
    _, groups, rows, width = up_codes.shape
    depth = down_codes.shape[-1]
    slots = (groups * width + depth) // LANES
    chips = rows // 2
    pairs = [[2 * q, 2 * q + 1] for q in range(chips)]
    sides = [[2 * q + c for q in range(chips)] for c in range(2)]
    sds = jax.ShapeDtypeStruct
    chunks = sds((rows, slots, LANES), jnp.bfloat16)
    up_exps = jnp.transpose(up_exps[0], (2, 0, 1))
    down_exps = jnp.transpose(down_exps[0], (1, 0))
    streamed = (code_table, up_codes[0], up_exps, down_codes[0], down_exps)
    decoded = pl.pallas_call(
        decode_kernel,
        compiler_params=PARAMS,
        out_shape=chunks,
        in_specs=[HBM] * 5,
        out_specs=VMEM,
        scratch_shapes=[
            pltpu.SMEM(code_table.shape, jnp.int32),
            pltpu.VMEM(up_codes.shape[1:], jnp.int32),
            pltpu.VMEM(up_exps.shape, jnp.int32),
            pltpu.VMEM(down_codes.shape[1:], jnp.int32),
            pltpu.VMEM(down_exps.shape, jnp.int32),
            pltpu.VMEM((rows * slots, LANES), jnp.int32),
            pltpu.VMEM((slots, rows), jnp.int32),
            pltpu.SemaphoreType.DMA((5,)),
        ],
    )(*[pltpu.with_memory_space_constraint(x, pltpu.HBM) for x in streamed])
    recv = lax.all_to_all(decoded, "replica", split_axis=0, concat_axis=0, axis_index_groups=sides, tiled=True)
    mine = pl.pallas_call(
        chip_sum_kernel,
        compiler_params=PARAMS,
        out_shape=sds((4, slots, LANES), jnp.float32),
        in_specs=[VMEM] * 5,
        out_specs=VMEM,
    )(recv, up_global, up_moment, down_global, down_moment)
    both = lax.all_gather(mine, "replica", axis=0, axis_index_groups=pairs, tiled=True)
    up_new, up_mom, down_new, down_mom, shared = pl.pallas_call(
        advance_kernel,
        compiler_params=PARAMS,
        out_shape=(
            sds(up_global.shape, jnp.float32),
            sds(up_global.shape, jnp.float32),
            sds(down_global.shape, jnp.float32),
            sds(down_global.shape, jnp.float32),
            chunks,
        ),
        in_specs=[VMEM],
        out_specs=(VMEM,) * 5,
        scratch_shapes=[pltpu.VMEM((2, slots, LANES), jnp.float32), pltpu.VMEM((2, slots, LANES), jnp.float32)],
    )(both)
    spread = lax.all_to_all(shared, "replica", split_axis=0, concat_axis=0, axis_index_groups=sides, tiled=True)
    up_merged, down_merged = pl.pallas_call(
        merge_kernel,
        compiler_params=PARAMS,
        out_shape=(sds(up_local.shape[1:], jnp.bfloat16), sds(down_local.shape[1:], jnp.bfloat16)),
        in_specs=[VMEM] * 3,
        out_specs=(VMEM,) * 2,
        scratch_shapes=[pltpu.VMEM((rows * slots, LANES), jnp.float32)],
    )(spread, up_local[0], down_local[0])
    return (up_new, up_mom, up_merged[None], down_new, down_mom, down_merged[None])


def solution(mesh):
    in_specs = (
        P(),
        P("replica", None, None, "mp"),
        P("replica", None, None, "mp"),
        P(None, "replica", "mp"),
        P(None, "replica", "mp"),
        P("replica", None, None, "mp"),
        P("replica", None, "mp"),
        P("replica", None, "mp"),
        P("replica", "mp"),
        P("replica", "mp"),
        P("replica", None, "mp"),
    )
    out_specs = (
        P(None, "replica", "mp"),
        P(None, "replica", "mp"),
        P("replica", None, None, "mp"),
        P("replica", "mp"),
        P("replica", "mp"),
        P("replica", None, "mp"),
    )
    return jax.shard_map(
        per_device, mesh=mesh, in_specs=in_specs, out_specs=out_specs, check_vma=False
    )
```

time: 48.8 us -> 41.3 us (0.85)
  blocking collectives: 42.5 us -> 37.3 us
  Pallas kernels: 5.39 us -> 2.83 us
    all_to_all x2, blocking collectives: 42.5 us -> 28.6 us  [the longest x1 18.3 us: per_device(): lax.all_to_all(decoded, 'replica', split_axis=0, concat_axis=0, axis_inde...]
    all_gather x0 -> x1, blocking collectives: none -> 8.66 us  [per_device(): lax.all_gather(mine, 'replica', axis=0, axis_index_groups=pairs, tiled=True)]
    pallas_call x3 -> x4, Pallas kernels: 5.39 us -> 2.83 us  [the longest x1 1.42 us: per_device(): pl.pallas_call(decode_kernel, compiler_params=PARAMS, out_shape=chunks, i...]
where the time goes in v2:
time: 41.3 us; the launch traced here: 40.8 us
  blocking collectives  37.3 us (90%)
  Pallas kernels  2.83 us (7%)
  between operations  0.69 us (2%)
    all_to_all x1, blocking collectives, per_device(): lax.all_to_all(decoded, 'replica', split_axis=0, concat_axis=0, axis_inde...  18.3 us
    all_to_all x1, blocking collectives, per_device(): lax.all_to_all(shared, 'replica', split_axis=0, concat_axis=0, axis_index...  10.3 us
    all_gather x1, blocking collectives, per_device(): lax.all_gather(mine, 'replica', axis=0, axis_index_groups=pairs, tiled=True)  8.66 us
    pallas_call x1, Pallas kernels, per_device(): pl.pallas_call(decode_kernel, compiler_params=PARAMS, out_shape=chunks, i...  1.42 us

profile of v2, /device:TPU:1, one launch (start us, length us, event | category | flops | bytes accessed | tf_op | source)
XLA Modules:
  0.0 40.8 jit_solution(13216652744074102428)
XLA Ops:
  0.6 1.4 %shard_map.154 = bf16[32,16,128]{2,1,0:T(8,128)(2,1)S(1)} custom-call(s32[16]{0:T(128)} %table_hbm.1, s32[2,32,896]{2,1,0:T(8,128)} %bitcast.14, s32[7,2,32]{2,1,0:T(2,128)} %bitcast.16, s32[32,256]{1,0:T(8,128)} %bitcast.15, s32[2,32]{1,0:T(2,128)} %bitcast.17), custom_call_target="tpu_custom_call" | custom-call | tf_op jit(solution)/shard_map/pallas_call | solution.py:156
  2.1 0.0 copy-start.2
  2.1 0.0 copy-start.3
  2.1 0.0 copy-start.4
  2.1 0.0 copy-start.5
  2.1 18.3 %all_to_all.10.recv = bf16[32,16,128]{2,1,0:T(8,128)(2,1)S(1)} all-to-all(bf16[32,16,128]{2,1,0:T(8,128)(2,1)S(1)} %shard_map.154), channel_id=1, replica_groups={{0,64,128,192,256,320,384,448,512,576,640,704,768,832,896,960},{32,96,1..., dimensions={0} | all-to-all | bytes 262144 | tf_op jit(solution)/shard_map/all_to_all | solution.py:173
  20.4 0.0 copy-done.2
  20.4 0.0 copy-done.3
  20.4 0.0 copy-done.4
  20.4 0.0 copy-done.5
  20.4 8.7 %all_gather.3.both = f32[8,16,128]{2,1,0:T(8,128)S(1)} all-gather(f32[4,16,128]{2,1,0:T(8,128)S(1)} %shard_map.155), channel_id=1, replica_groups={{0,32},{64,96},{128,160},{192,224},{256,288},{320,352},{384,416},{448,4..., dimensions={0}, use_global_device_ids=true | all-gather | bytes 98304 | tf_op jit(solution)/shard_map/all_gather | solution.py:181
  29.1 0.6 %shard_map.156 = (f32[2,1,896]{2,1,0:T(1,128)}, f32[2,1,896]{2,1,0:T(1,128)}, f32[1,256]{1,0:T(1,128)}, f32[1,256]{1,0:T(1,128)}, bf16[32,16,128]{2,1,0:T(8,128)(2,1)S(1)}) custom-call(f32[8,16,128]{2,1,0:T(8,128)S(1)} %all_gather.3.both), custom_call_target="tpu_custom_call" | custom-call | tf_op jit(solution)/shard_map/pallas_call | solution.py:182
  29.7 0.0 copy-start
  29.7 0.0 copy-start.1
  29.7 10.3 %all_to_all.11.recv = bf16[32,16,128]{2,1,0:T(8,128)(2,1)S(1)} all-to-all(bf16[32,16,128]{2,1,0:T(8,128)(2,1)S(1)} %get-tuple-element.15), channel_id=1, replica_groups={{0,64,128,192,256,320,384,448,512,576,640,704,768,832,896,960},{32,96,1..., dimensions={0} | all-to-all | bytes 262144 | tf_op jit(solution)/shard_map/all_to_all | solution.py:196
  40.1 0.0 copy-done
  40.1 0.0 copy-done.1
  40.1 0.8 %shard_map.157 = (bf16[2,32,896]{2,1,0:T(8,128)(2,1)}, bf16[32,256]{1,0:T(8,128)(2,1)}) custom-call(bf16[32,16,128]{2,1,0:T(8,128)(2,1)S(1)} %all_to_all.11.recv, bf16[2,32,896]{2,1,0:T(8,128)(2,1)S(1)} %bitcast.12, bf16[32,256]{1,0:T(8,128)(2,1)S(1)} %bitcast.13), custom_call_target="tpu_custom_call" | custom-call | tf_op jit(solution)/shard_map/pallas_call | solution.py:197
  (1 shorter events, 0.0 us)
Async XLA Ops:
  2.1 18.3 %copy-start.2 = (f32[2,1,896]{2,1,0:T(1,128)S(1)}, f32[2,1,896]{2,1,0:T(1,128)}, u32[]{:S(2)}) copy-start(f32[2,1,896]{2,1,0:T(1,128)} %up_global.1) | copy-start | bytes 21508
  2.1 18.3 %copy-start.3 = (f32[2,1,896]{2,1,0:T(1,128)S(1)}, f32[2,1,896]{2,1,0:T(1,128)}, u32[]{:S(2)}) copy-start(f32[2,1,896]{2,1,0:T(1,128)} %up_moment.1) | copy-start | bytes 21508
  2.1 18.3 %copy-start.4 = (f32[1,256]{1,0:T(1,128)S(1)}, f32[1,256]{1,0:T(1,128)}, u32[]{:S(2)}) copy-start(f32[1,256]{1,0:T(1,128)} %down_global.1) | copy-start | bytes 3076
  2.1 18.3 %copy-start.5 = (f32[1,256]{1,0:T(1,128)S(1)}, f32[1,256]{1,0:T(1,128)}, u32[]{:S(2)}) copy-start(f32[1,256]{1,0:T(1,128)} %down_moment.1) | copy-start | bytes 3076
  29.7 10.3 %copy-start = (bf16[1,2,32,896]{3,2,1,0:T(8,128)(2,1)S(1)}, bf16[1,2,32,896]{3,2,1,0:T(8,128)(2,1)}, u32[]{:S(2)}) copy-start(bf16[1,2,32,896]{3,2,1,0:T(8,128)(2,1)} %param.16) | copy-start | bytes 344068
  29.7 10.3 %copy-start.1 = (bf16[1,32,256]{2,1,0:T(8,128)(2,1)S(1)}, bf16[1,32,256]{2,1,0:T(8,128)(2,1)}, u32[]{:S(2)}) copy-start(bf16[1,32,256]{2,1,0:T(8,128)(2,1)} %param.21) | copy-start | bytes 49156

commit v3 on v2

--- a/solution.py
+++ b/solution.py
@@ -86,7 +86,7 @@
         out_ref[3, j : j + 1, :] = down_moment[:, t * LANES : (t + 1) * LANES]
 
 
-def advance_kernel(both, up_new, up_mom, down_new, down_mom, out_ref, weights, moment):
+def advance_kernel(both, out_ref, state, rows_new):
     core = lax.rem(lax.axis_index("replica"), 2)
     replicas = out_ref.shape[0]
     for k in range(2):
@@ -96,20 +96,14 @@
         shared = weights_new.astype(jnp.bfloat16)
         for q in range(replicas // 2):
             out_ref[2 * q + k] = shared
-        weights[k] = weights_new
-        moment[k] = moment_new
-    groups, _, width = up_new.shape
-    up_blocks = width // LANES
-    for j, g, s in up_slots(groups, up_blocks):
-        up_new[g, :, s * LANES : (s + 1) * LANES] = weights[core, j : j + 1, :]
-        up_mom[g, :, s * LANES : (s + 1) * LANES] = moment[core, j : j + 1, :]
-    for t in range(down_new.shape[1] // LANES):
-        j = groups * up_blocks + t
-        down_new[:, t * LANES : (t + 1) * LANES] = weights[core, j : j + 1, :]
-        down_mom[:, t * LANES : (t + 1) * LANES] = moment[core, j : j + 1, :]
-
-
-def merge_kernel(recv, up_local, down_local, up_merged, down_merged, shared):
+        rows_new[k, 0] = weights_new
+        rows_new[k, 1] = moment_new
+    state[...] = rows_new[core]
+
+
+def merge_kernel(
+    recv, up_local, down_local, state, up_merged, down_merged, up_new, up_mom, down_new, down_mom, shared
+):
     groups, rows, width = up_local.shape
     up_blocks = width // LANES
     down_blocks = down_local.shape[1] // LANES
@@ -122,11 +116,16 @@
         return (mixing * local.astype(jnp.float32) + (1.0 - mixing) * theirs).astype(jnp.bfloat16)
 
     for j, g, s in up_slots(groups, up_blocks):
-        at = (g, slice(None), slice(s * LANES, (s + 1) * LANES))
-        up_merged[at] = merged(up_local[at], j)
+        lanes = slice(s * LANES, (s + 1) * LANES)
+        up_merged[g, :, lanes] = merged(up_local[g, :, lanes], j)
+        up_new[g, :, lanes] = state[0, j : j + 1, :]
+        up_mom[g, :, lanes] = state[1, j : j + 1, :]
     for t in range(down_blocks):
-        at = (slice(None), slice(t * LANES, (t + 1) * LANES))
-        down_merged[at] = merged(down_local[at], groups * up_blocks + t)
+        j = groups * up_blocks + t
+        lanes = slice(t * LANES, (t + 1) * LANES)
+        down_merged[:, lanes] = merged(down_local[:, lanes], j)
+        down_new[:, lanes] = state[0, j : j + 1, :]
+        down_mom[:, lanes] = state[1, j : j + 1, :]
 
 
 def per_device(
@@ -179,29 +178,30 @@
         out_specs=VMEM,
     )(recv, up_global, up_moment, down_global, down_moment)
     both = lax.all_gather(mine, "replica", axis=0, axis_index_groups=pairs, tiled=True)
-    up_new, up_mom, down_new, down_mom, shared = pl.pallas_call(
+    shared, state = pl.pallas_call(
         advance_kernel,
         compiler_params=PARAMS,
+        out_shape=(chunks, sds((2, slots, LANES), jnp.float32)),
+        in_specs=[VMEM],
+        out_specs=(VMEM,) * 2,
+        scratch_shapes=[pltpu.VMEM((2, 2, slots, LANES), jnp.float32)],
+    )(both)
+    spread = lax.all_to_all(shared, "replica", split_axis=0, concat_axis=0, axis_index_groups=sides, tiled=True)
+    up_merged, down_merged, up_new, up_mom, down_new, down_mom = pl.pallas_call(
+        merge_kernel,
+        compiler_params=PARAMS,
         out_shape=(
+            sds(up_local.shape[1:], jnp.bfloat16),
+            sds(down_local.shape[1:], jnp.bfloat16),
             sds(up_global.shape, jnp.float32),
             sds(up_global.shape, jnp.float32),
             sds(down_global.shape, jnp.float32),
             sds(down_global.shape, jnp.float32),
-            chunks,
         ),
-        in_specs=[VMEM],
-        out_specs=(VMEM,) * 5,
-        scratch_shapes=[pltpu.VMEM((2, slots, LANES), jnp.float32), pltpu.VMEM((2, slots, LANES), jnp.float32)],
-    )(both)
-    spread = lax.all_to_all(shared, "replica", split_axis=0, concat_axis=0, axis_index_groups=sides, tiled=True)
-    up_merged, down_merged = pl.pallas_call(
-        merge_kernel,
-        compiler_params=PARAMS,
-        out_shape=(sds(up_local.shape[1:], jnp.bfloat16), sds(down_local.shape[1:], jnp.bfloat16)),
-        in_specs=[VMEM] * 3,
-        out_specs=(VMEM,) * 2,
+        in_specs=[VMEM] * 4,
+        out_specs=(VMEM,) * 6,
         scratch_shapes=[pltpu.VMEM((rows * slots, LANES), jnp.float32)],
-    )(spread, up_local[0], down_local[0])
+    )(spread, up_local[0], down_local[0], state)
     return (up_new, up_mom, up_merged[None], down_new, down_mom, down_merged[None])
 
 

time: 41.3 us -> 40.8 us (0.988)
  Pallas kernels: 2.83 us -> 2.25 us
    pallas_call x1, Pallas kernels: 0.63 us -> 0.02 us  [per_device(): pl.pallas_call(advance_kernel, compiler_params=PARAMS, out_shape=(chunks,...]
where the time goes in v3:
time: 40.8 us; the launch traced here: 40.3 us
  blocking collectives  37.3 us (91%)
  Pallas kernels  2.25 us (6%)
  between operations  0.71 us (2%)
    all_to_all x1, blocking collectives, per_device(): lax.all_to_all(decoded, 'replica', split_axis=0, concat_axis=0, axis_inde...  18.3 us
    all_to_all x1, blocking collectives, per_device(): lax.all_to_all(shared, 'replica', split_axis=0, concat_axis=0, axis_index...  10.3 us
    all_gather x1, blocking collectives, per_device(): lax.all_gather(mine, 'replica', axis=0, axis_index_groups=pairs, tiled=True)  8.66 us
    pallas_call x1, Pallas kernels, per_device(): pl.pallas_call(decode_kernel, compiler_params=PARAMS, out_shape=chunks, i...  1.42 us

profile of v3, /device:TPU:1, one launch (start us, length us, event | category | flops | bytes accessed | tf_op | source)
XLA Modules:
  0.0 40.3 jit_solution(6487802019182460095)
XLA Ops:
  0.6 1.4 %shard_map.154 = bf16[32,16,128]{2,1,0:T(8,128)(2,1)S(1)} custom-call(s32[16]{0:T(128)} %table_hbm.1, s32[2,32,896]{2,1,0:T(8,128)} %bitcast.14, s32[7,2,32]{2,1,0:T(2,128)} %bitcast.16, s32[32,256]{1,0:T(8,128)} %bitcast.15, s32[2,32]{1,0:T(2,128)} %bitcast.17), custom_call_target="tpu_custom_call" | custom-call | tf_op jit(solution)/shard_map/pallas_call | solution.py:155
  2.1 0.0 copy-start.2
  2.1 0.0 copy-start.3
  2.1 0.0 copy-start.4
  2.1 0.0 copy-start.5
  2.1 18.3 %all_to_all.10.recv = bf16[32,16,128]{2,1,0:T(8,128)(2,1)S(1)} all-to-all(bf16[32,16,128]{2,1,0:T(8,128)(2,1)S(1)} %shard_map.154), channel_id=1, replica_groups={{0,64,128,192,256,320,384,448,512,576,640,704,768,832,896,960},{32,96,1..., dimensions={0} | all-to-all | bytes 262144 | tf_op jit(solution)/shard_map/all_to_all | solution.py:172
  20.4 0.0 copy-done.2
  20.4 0.0 copy-done.3
  20.4 0.0 copy-done.4
  20.4 0.0 copy-done.5
  20.4 8.7 %all_gather.3.both = f32[8,16,128]{2,1,0:T(8,128)S(1)} all-gather(f32[4,16,128]{2,1,0:T(8,128)S(1)} %shard_map.155), channel_id=1, replica_groups={{0,32},{64,96},{128,160},{192,224},{256,288},{320,352},{384,416},{448,4..., dimensions={0}, use_global_device_ids=true | all-gather | bytes 98304 | tf_op jit(solution)/shard_map/all_gather | solution.py:180
  29.1 0.0 copy-start
  29.1 0.0 copy-start.1
  29.2 10.3 %all_to_all.11.recv = bf16[32,16,128]{2,1,0:T(8,128)(2,1)S(1)} all-to-all(bf16[32,16,128]{2,1,0:T(8,128)(2,1)S(1)} %get-tuple-element.14), channel_id=1, replica_groups={{0,64,128,192,256,320,384,448,512,576,640,704,768,832,896,960},{32,96,1..., dimensions={0} | all-to-all | bytes 262144 | tf_op jit(solution)/shard_map/all_to_all | solution.py:189
  39.5 0.0 copy-done
  39.5 0.0 copy-done.1
  39.5 0.8 %shard_map.157 = (bf16[2,32,896]{2,1,0:T(8,128)(2,1)}, bf16[32,256]{1,0:T(8,128)(2,1)}, f32[2,1,896]{2,1,0:T(1,128)}, f32[2,1,896]{2,1,0:T(1,128)}, f32[1,256]{1,0:T(1,128)}, /*index=5*/f32[1,256]{1,0:T(1,128)}) custom-call(bf16[32,16,128]{2,1,0:T(8,128)(2,1)S(1)} %all_to_all.11.recv, bf16[2,32,896]{2,1,0:T(8,128)(2,1)S(1)} %bitcast.12, ...), custom_call_target="tpu_custom_call" | custom-call | tf_op jit(solution)/shard_map/pallas_call | solution.py:190
  (2 shorter events, 0.0 us)
Async XLA Ops:
  2.1 18.3 %copy-start.2 = (f32[2,1,896]{2,1,0:T(1,128)S(1)}, f32[2,1,896]{2,1,0:T(1,128)}, u32[]{:S(2)}) copy-start(f32[2,1,896]{2,1,0:T(1,128)} %up_global.1) | copy-start | bytes 21508
  2.1 18.3 %copy-start.3 = (f32[2,1,896]{2,1,0:T(1,128)S(1)}, f32[2,1,896]{2,1,0:T(1,128)}, u32[]{:S(2)}) copy-start(f32[2,1,896]{2,1,0:T(1,128)} %up_moment.1) | copy-start | bytes 21508
  2.1 18.3 %copy-start.4 = (f32[1,256]{1,0:T(1,128)S(1)}, f32[1,256]{1,0:T(1,128)}, u32[]{:S(2)}) copy-start(f32[1,256]{1,0:T(1,128)} %down_global.1) | copy-start | bytes 3076
  2.1 18.3 %copy-start.5 = (f32[1,256]{1,0:T(1,128)S(1)}, f32[1,256]{1,0:T(1,128)}, u32[]{:S(2)}) copy-start(f32[1,256]{1,0:T(1,128)} %down_moment.1) | copy-start | bytes 3076
  29.1 10.4 %copy-start = (bf16[1,2,32,896]{3,2,1,0:T(8,128)(2,1)S(1)}, bf16[1,2,32,896]{3,2,1,0:T(8,128)(2,1)}, u32[]{:S(2)}) copy-start(bf16[1,2,32,896]{3,2,1,0:T(8,128)(2,1)} %param.16) | copy-start | bytes 344068
  29.1 10.4 %copy-start.1 = (bf16[1,32,256]{2,1,0:T(8,128)(2,1)S(1)}, bf16[1,32,256]{2,1,0:T(8,128)(2,1)}, u32[]{:S(2)}) copy-start(bf16[1,32,256]{2,1,0:T(8,128)(2,1)} %param.21) | copy-start | bytes 49156

commit v4 on v3

v4 whole, which is shorter than its diff:
```python
import jax
import jax.numpy as jnp
from jax import lax
from jax.experimental import pallas as pl
from jax.experimental.pallas import tpu as pltpu
from jax.sharding import PartitionSpec as P

LANES = 128
LOW_EXP = -8

outer_rate = 0.7
nesterov = 0.9
mixing = 0.5

VMEM = pl.BlockSpec(memory_space=pltpu.VMEM)
HBM = pl.BlockSpec(memory_space=pltpu.HBM)


PARAMS = pltpu.CompilerParams(vmem_limit_bytes=4 * 1024 * 1024)


def up_slots(groups, blocks):
    return [(s * groups + g, g, s) for s in range(blocks) for g in range(groups)]


def pieces_of(x):
    high = x.astype(jnp.bfloat16)
    rest = x - high.astype(jnp.float32)
    middle = rest.astype(jnp.bfloat16)
    low = (rest - middle.astype(jnp.float32)).astype(jnp.bfloat16)
    return [high, middle, low]


def sum_of(ref, first):
    high, middle, low = [ref[first + i].astype(jnp.float32) for i in range(3)]
    return (high + middle) + low


def decode_kernel(
    table_hbm, up_exps_hbm, down_exps_hbm, up_global_hbm, up_moment_hbm, down_global_hbm, down_moment_hbm,
    down_codes_hbm, up_codes_hbm, out_ref,
    table_ref, up_exps, down_exps, up_global, up_moment, down_global, down_moment, down_codes, up_codes,
    codes_by_row, exps_by_slot, owned, sems,
):
    sources = [
        table_hbm, up_exps_hbm, down_exps_hbm, up_global_hbm, up_moment_hbm, down_global_hbm, down_moment_hbm,
        down_codes_hbm, up_codes_hbm,
    ]
    targets = [
        table_ref, up_exps, down_exps, up_global, up_moment, down_global, down_moment, down_codes, up_codes,
    ]
    copies = [pltpu.make_async_copy(a, b, sems.at[i]) for i, (a, b) in enumerate(zip(sources, targets))]
    for copy in reversed(copies):
        copy.start()
    groups, rows, width = up_codes.shape
    up_blocks = width // LANES
    down_blocks = down_codes.shape[1] // LANES
    slots = groups * up_blocks + down_blocks
    copies[0].wait()
    lane = lax.broadcasted_iota(jnp.int32, (slots, LANES), 1)
    table = jnp.zeros((slots, LANES), jnp.int32)
    for level in range(16):
        table = jnp.where(lane == level, table_ref[level], table)
    table = table.astype(jnp.float32)
    for copy in copies[1:-1]:
        copy.wait()
    for j, g, s in up_slots(groups, up_blocks):
        lanes = slice(s * LANES, (s + 1) * LANES)
        exps_by_slot[j : j + 1, :] = up_exps[s, g : g + 1, :]
        owned[0, j : j + 1, :] = up_global[g, :, lanes]
        owned[1, j : j + 1, :] = up_moment[g, :, lanes]
    for t in range(down_blocks):
        j = groups * up_blocks + t
        lanes = slice(t * LANES, (t + 1) * LANES)
        codes_by_row[pl.ds(j, rows, stride=slots), :] = down_codes[:, lanes]
        exps_by_slot[j : j + 1, :] = down_exps[t : t + 1, :]
        owned[0, j : j + 1, :] = down_global[:, lanes]
        owned[1, j : j + 1, :] = down_moment[:, lanes]
    for k in range(2):
        for i, piece in enumerate(pieces_of(owned[k])):
            out_ref[rows + 3 * k + i] = piece
    scales = jnp.left_shift(1, exps_by_slot[...] - LOW_EXP).astype(jnp.float32) * 2.0**LOW_EXP
    copies[-1].wait()
    for j, g, s in up_slots(groups, up_blocks):
        codes_by_row[pl.ds(j, rows, stride=slots), :] = up_codes[g, :, s * LANES : (s + 1) * LANES]
    for r in range(rows):
        codes = codes_by_row[r * slots : (r + 1) * slots, :]
        values = jnp.take_along_axis(table, codes, axis=1)
        out_ref[r] = (values * scales[:, r : r + 1]).astype(jnp.bfloat16)


def pair_kernel(both, out_ref):
    rows = out_ref.shape[0]
    step = both.shape[0] // 2
    for r in range(rows):
        total = both[r].astype(jnp.float32) + both[step + r].astype(jnp.float32)
        out_ref[r] = (total * 2.0**-LOW_EXP).astype(jnp.int32).astype(jnp.int16)


def advanced(mean, weights, moment):
    moment_new = nesterov * moment + mean
    return weights - outer_rate * (mean + nesterov * moment_new), moment_new


def advance_kernel(recv, both, out_ref, totals):
    replicas = out_ref.shape[0]
    step = both.shape[0] // 2
    for k in range(2):
        total = recv[k].astype(jnp.int32)
        for q in range(1, replicas // 2):
            total = total + recv[2 * q + k].astype(jnp.int32)
        total = total.astype(jnp.float32)
        first = step * k + replicas
        mean = total * (2.0**LOW_EXP / replicas)
        weights_new, _ = advanced(mean, sum_of(both, first), sum_of(both, first + 3))
        shared = weights_new.astype(jnp.bfloat16)
        for q in range(replicas // 2):
            out_ref[2 * q + k] = shared
        high = total.astype(jnp.bfloat16)
        totals[2 * k] = high
        totals[2 * k + 1] = (total - high.astype(jnp.float32)).astype(jnp.bfloat16)


def join_kernel(spread, totals, out_ref):
    rows = spread.shape[0]
    out_ref[0:rows] = spread[...]
    out_ref[rows:] = totals[...]


def merge_kernel(
    both, decoded, up_local, down_local, up_merged, down_merged, up_new, up_mom, down_new, down_mom, shared, state
):
    groups, rows, width = up_local.shape
    up_blocks = width // LANES
    down_blocks = down_local.shape[1] // LANES
    step, slots = both.shape[0] // 2, both.shape[1]
    core = lax.rem(lax.axis_index("replica"), 2)
    first = step + rows + 2 * core
    total = both[first].astype(jnp.float32) + both[first + 1].astype(jnp.float32)
    mean = total * (2.0**LOW_EXP / rows)
    state[0], state[1] = advanced(mean, sum_of(decoded, rows), sum_of(decoded, rows + 3))
    for r in range(rows):
        shared[r * slots : (r + 1) * slots, :] = both[step + r].astype(jnp.float32)

    def merged(local, j):
        theirs = shared[pl.ds(j, rows, stride=slots), :]
        return (mixing * local.astype(jnp.float32) + (1.0 - mixing) * theirs).astype(jnp.bfloat16)

    for j, g, s in up_slots(groups, up_blocks):
        lanes = slice(s * LANES, (s + 1) * LANES)
        up_merged[g, :, lanes] = merged(up_local[g, :, lanes], j)
        up_new[g, :, lanes] = state[0, j : j + 1, :]
        up_mom[g, :, lanes] = state[1, j : j + 1, :]
    for t in range(down_blocks):
        j = groups * up_blocks + t
        lanes = slice(t * LANES, (t + 1) * LANES)
        down_merged[:, lanes] = merged(down_local[:, lanes], j)
        down_new[:, lanes] = state[0, j : j + 1, :]
        down_mom[:, lanes] = state[1, j : j + 1, :]


def per_device(
    code_table,
    up_codes,
    up_exps,
    up_global,
    up_moment,
    up_local,
    down_codes,
    down_exps,
    down_global,
    down_moment,
    down_local,
):
    _, groups, rows, width = up_codes.shape
    depth = down_codes.shape[-1]
    slots = (groups * width + depth) // LANES
    chips = rows // 2
    pairs = [[2 * q, 2 * q + 1] for q in range(chips)]
    sides = [[2 * q + c for q in range(chips)] for c in range(2)]
    core = lax.rem(lax.axis_index("replica"), 2)
    sds = jax.ShapeDtypeStruct

    def across(x):
        return lax.cond(
            core == 1,
            lambda v: lax.all_to_all(v, "replica", split_axis=0, concat_axis=0, axis_index_groups=sides, tiled=True),
            lambda v: v,
            x,
        )

    streamed = (
        code_table,
        jnp.transpose(up_exps[0], (2, 0, 1)),
        jnp.transpose(down_exps[0], (1, 0)),
        up_global,
        up_moment,
        down_global,
        down_moment,
        down_codes[0],
        up_codes[0],
    )
    decoded = pl.pallas_call(
        decode_kernel,
        compiler_params=PARAMS,
        out_shape=sds((rows + 6, slots, LANES), jnp.bfloat16),
        in_specs=[HBM] * len(streamed),
        out_specs=VMEM,
        scratch_shapes=[
            pltpu.SMEM(code_table.shape, jnp.int32),
            *[pltpu.VMEM(x.shape, x.dtype) for x in streamed[1:]],
            pltpu.VMEM((rows * slots, LANES), jnp.int32),
            pltpu.VMEM((slots, rows), jnp.int32),
            pltpu.VMEM((2, slots, LANES), jnp.float32),
            pltpu.SemaphoreType.DMA((len(streamed),)),
        ],
    )(*[pltpu.with_memory_space_constraint(x, pltpu.HBM) for x in streamed])
    both = lax.all_gather(decoded, "replica", axis=0, axis_index_groups=pairs, tiled=True)
    sums = pl.pallas_call(
        pair_kernel,
        compiler_params=PARAMS,
        out_shape=sds((rows, slots, LANES), jnp.int16),
        in_specs=[VMEM],
        out_specs=VMEM,
    )(both)
    recv = across(sums)
    shared, totals = pl.pallas_call(
        advance_kernel,
        compiler_params=PARAMS,
        out_shape=(sds((rows, slots, LANES), jnp.bfloat16), sds((4, slots, LANES), jnp.bfloat16)),
        in_specs=[VMEM] * 2,
        out_specs=(VMEM,) * 2,
    )(recv, both)
    spread = across(shared)
    joined = pl.pallas_call(
        join_kernel,
        compiler_params=PARAMS,
        out_shape=sds((rows + 4, slots, LANES), jnp.bfloat16),
        in_specs=[VMEM] * 2,
        out_specs=VMEM,
    )(spread, totals)
    final = lax.all_gather(joined, "replica", axis=0, axis_index_groups=pairs, tiled=True)
    up_merged, down_merged, up_new, up_mom, down_new, down_mom = pl.pallas_call(
        merge_kernel,
        compiler_params=PARAMS,
        out_shape=(
            sds(up_local.shape[1:], jnp.bfloat16),
            sds(down_local.shape[1:], jnp.bfloat16),
            sds(up_global.shape, jnp.float32),
            sds(up_global.shape, jnp.float32),
            sds(down_global.shape, jnp.float32),
            sds(down_global.shape, jnp.float32),
        ),
        in_specs=[VMEM] * 4,
        out_specs=(VMEM,) * 6,
        scratch_shapes=[pltpu.VMEM((rows * slots, LANES), jnp.float32), pltpu.VMEM((2, slots, LANES), jnp.float32)],
    )(final, decoded, up_local[0], down_local[0])
    return (up_new, up_mom, up_merged[None], down_new, down_mom, down_merged[None])


def solution(mesh):
    in_specs = (
        P(),
        P("replica", None, None, "mp"),
        P("replica", None, None, "mp"),
        P(None, "replica", "mp"),
        P(None, "replica", "mp"),
        P("replica", None, None, "mp"),
        P("replica", None, "mp"),
        P("replica", None, "mp"),
        P("replica", "mp"),
        P("replica", "mp"),
        P("replica", None, "mp"),
    )
    out_specs = (
        P(None, "replica", "mp"),
        P(None, "replica", "mp"),
        P("replica", None, None, "mp"),
        P("replica", "mp"),
        P("replica", "mp"),
        P("replica", None, "mp"),
    )
    return jax.shard_map(
        per_device, mesh=mesh, in_specs=in_specs, out_specs=out_specs, check_vma=False
    )
```

time: 40.8 us -> 41.4 us (1.015)
  blocking collectives: 37.3 us -> 38.2 us
    all_gather x1 -> x2, blocking collectives: 8.66 us -> 18 us  [the longest x1 15.8 us: per_device(): lax.all_gather(decoded, 'replica', axis=0, axis_index_groups=pairs, tiled...]
    all_to_all x2, blocking collectives: 28.6 us -> 20.2 us  [across(): lax.all_to_all(v, 'replica', split_axis=0, concat_axis=0, axis_index_grou...]
    pallas_call x3 -> x4, Pallas kernels: 1.47 us -> 1.53 us  [the longest x1 1.41 us: per_device(): pl.pallas_call(decode_kernel, compiler_params=PARAMS, out_shape=sds((rows...]
where the time goes in v4:
time: 41.4 us; the launch traced here: 41.3 us
  blocking collectives  38.2 us (92%)
  Pallas kernels  2.32 us (6%)
  between operations  0.68 us (2%)
    all_to_all x2, blocking collectives, across(): lax.all_to_all(v, 'replica', split_axis=0, concat_axis=0, axis_index_grou...  20.2 us
    all_gather x1, blocking collectives, per_device(): lax.all_gather(decoded, 'replica', axis=0, axis_index_groups=pairs, tiled...  15.8 us
    all_gather x1, blocking collectives, per_device(): lax.all_gather(joined, 'replica', axis=0, axis_index_groups=pairs, tiled=...  2.15 us
    pallas_call x1, Pallas kernels, per_device(): pl.pallas_call(decode_kernel, compiler_params=PARAMS, out_shape=sds((rows...  1.41 us

profile of v4, /device:TPU:1, one launch (start us, length us, event | category | flops | bytes accessed | tf_op | source)
XLA Modules:
  0.0 41.3 jit_solution(4290504216981798204)
XLA Ops:
  0.6 1.4 %shard_map.154.decoded = bf16[38,16,128]{2,1,0:T(8,128)(2,1)S(1)} custom-call(s32[16]{0:T(128)} %table_hbm.1, s32[7,2,32]{2,1,0:T(2,128)} %bitcast.16, s32[2,32]{1,0:T(2,128)} %bitcast.17, f32[2,1,896]{2,1,0:T(1,128)} %up_global_hbm.1, f32[2,1,896]{2,1,0:T(1,128)} %up_moment_hbm.1, f32[1,256]{1,0:T(1,128)} %down_global_hbm.1, f32[1,256]{1,0:T(1,128)} %down_moment_hbm.1, ...), custom_call_target="tpu_custom_call" | custom-call | tf_op jit(solution)/shard_map/pallas_call | solution.py:203
  2.1 15.8 %all_gather.6.both = bf16[76,16,128]{2,1,0:T(8,128)(2,1)S(1)} all-gather(bf16[38,16,128]{2,1,0:T(8,128)(2,1)S(1)} %shard_map.154.decoded), channel_id=1, replica_groups={{0,32},{64,96},{128,160},{192,224},{256,288},{320,352},{384,416},{448,4..., dimensions={0}, use_global_device_ids=true | all-gather | bytes 466944 | tf_op jit(solution)/shard_map/all_gather | solution.py:218
  17.9 0.1 shard_map.155
  17.9 10.0 %conditional.2 = (s16[32,16,128]{2,1,0:T(8,128)(2,1)S(1)}) conditional(s32[]{:T(128)} %convert_element_type.4, s16[32,16,128]{2,1,0:T(8,128)(2,1)S(1)} %shard_map.155, s16[32,16,128]{2,1,0:T(8,128)(2,1)S(1)} %shard_map.155), branch_computations={%region_0.0_spmd, %region_1.0_spmd} | conditional | bytes 524296 | solution.py:185
  18.0 10.0 %all_to_all.8 = s16[32,16,128]{2,1,0:T(8,128)(2,1)S(1)} all-to-all(s16[32,16,128]{2,1,0:T(8,128)(2,1)S(1)} %copy.21), channel_id=1, replica_groups={{0,64,128,192,256,320,384,448,512,576,640,704,768,832,896,960},{32,96,1..., dimensions={0} | all-to-all | bytes 262144 | tf_op jit(solution)/shard_map/cond/branch_1_fun/all_to_all | solution.py:187
  28.0 10.2 %conditional.3 = (bf16[32,16,128]{2,1,0:T(8,128)(2,1)S(1)}) conditional(s32[]{:T(128)} %convert_element_type.4, bf16[32,16,128]{2,1,0:T(8,128)(2,1)S(1)} %get-tuple-element.24, bf16[32,16,128]{2,1,0:T(8,128)(2,1)S(1)} %get-tuple-element.24), branch_computations={%region_2.0_spmd, %region_3.0_spmd} | conditional | bytes 524296 | solution.py:185
  28.1 10.2 %all_to_all.9 = bf16[32,16,128]{2,1,0:T(8,128)(2,1)S(1)} all-to-all(bf16[32,16,128]{2,1,0:T(8,128)(2,1)S(1)} %copy.22), channel_id=1, replica_groups={{0,64,128,192,256,320,384,448,512,576,640,704,768,832,896,960},{32,96,1..., dimensions={0} | all-to-all | bytes 262144 | tf_op jit(solution)/shard_map/cond/branch_1_fun/all_to_all | solution.py:187
  38.3 0.0 copy-start
  38.3 0.0 copy-start.1
  38.3 2.1 %all_gather.7.both = bf16[72,16,128]{2,1,0:T(8,128)(2,1)S(1)} all-gather(bf16[36,16,128]{2,1,0:T(8,128)(2,1)S(1)} %shard_map.157), channel_id=1, replica_groups={{0,32},{64,96},{128,160},{192,224},{256,288},{320,352},{384,416},{448,4..., dimensions={0}, use_global_device_ids=true | all-gather | bytes 442368 | tf_op jit(solution)/shard_map/all_gather | solution.py:242
  40.5 0.0 copy-done
  40.5 0.0 copy-done.1
  40.5 0.8 %shard_map.158 = (bf16[2,32,896]{2,1,0:T(8,128)(2,1)}, bf16[32,256]{1,0:T(8,128)(2,1)}, f32[2,1,896]{2,1,0:T(1,128)}, f32[2,1,896]{2,1,0:T(1,128)}, f32[1,256]{1,0:T(1,128)}, /*index=5*/f32[1,256]{1,0:T(1,128)}) custom-call(bf16[72,16,128]{2,1,0:T(8,128)(2,1)S(1)} %all_gather.7.both, bf16[38,16,128]{2,1,0:T(8,128)(2,1)S(1)} %shard_map.154.decoded, ...), custom_call_target="tpu_custom_call" | custom-call | tf_op jit(solution)/shard_map/pallas_call | solution.py:243
  (4 shorter events, 0.1 us)
Async XLA Ops:
  38.3 2.2 %copy-start = (bf16[1,2,32,896]{3,2,1,0:T(8,128)(2,1)S(1)}, bf16[1,2,32,896]{3,2,1,0:T(8,128)(2,1)}, u32[]{:S(2)}) copy-start(bf16[1,2,32,896]{3,2,1,0:T(8,128)(2,1)} %param.20) | copy-start | bytes 344068
  38.3 2.2 %copy-start.1 = (bf16[1,32,256]{2,1,0:T(8,128)(2,1)S(1)}, bf16[1,32,256]{2,1,0:T(8,128)(2,1)}, u32[]{:S(2)}) copy-start(bf16[1,32,256]{2,1,0:T(8,128)(2,1)} %param.25) | copy-start | bytes 49156

commit v5 on v3

--- a/solution.py
+++ b/solution.py
@@ -39,18 +39,14 @@
             ]
         )
     ]
-    for copy in copies:
+    for copy in reversed(copies):
         copy.start()
     groups, rows, width = up_codes.shape
     up_blocks = width // LANES
     down_blocks = down_codes.shape[1] // LANES
     slots = groups * up_blocks + down_blocks
     copies[0].wait()
-    lane = lax.broadcasted_iota(jnp.int32, (slots, LANES), 1)
-    table = jnp.zeros((slots, LANES), jnp.int32)
-    for level in range(16):
-        table = jnp.where(lane == level, table_ref[level], table)
-    table = table.astype(jnp.float32)
+    table = [table_ref[level].astype(jnp.float32) for level in range(16)]
     for copy in copies[1:4]:
         copy.wait()
     for j, g, s in up_slots(groups, up_blocks):
@@ -65,7 +61,11 @@
         codes_by_row[pl.ds(j, rows, stride=slots), :] = up_codes[g, :, s * LANES : (s + 1) * LANES]
     for r in range(rows):
         codes = codes_by_row[r * slots : (r + 1) * slots, :]
-        values = jnp.take_along_axis(table, codes, axis=1)
+        values = table
+        for bit in range(4):
+            odd = (codes & (1 << bit)) != 0
+            values = [jnp.where(odd, values[i + 1], values[i]) for i in range(0, len(values), 2)]
+        values = values[0]
         out_ref[r] = (values * scales[:, r : r + 1]).astype(jnp.bfloat16)
 
 
@@ -147,6 +147,7 @@
     chips = rows // 2
     pairs = [[2 * q, 2 * q + 1] for q in range(chips)]
     sides = [[2 * q + c for q in range(chips)] for c in range(2)]
+    first_sides = [[1 - c] + side[1:] for c, side in enumerate(sides)]
     sds = jax.ShapeDtypeStruct
     chunks = sds((rows, slots, LANES), jnp.bfloat16)
     up_exps = jnp.transpose(up_exps[0], (2, 0, 1))
@@ -169,7 +170,9 @@
             pltpu.SemaphoreType.DMA((5,)),
         ],
     )(*[pltpu.with_memory_space_constraint(x, pltpu.HBM) for x in streamed])
-    recv = lax.all_to_all(decoded, "replica", split_axis=0, concat_axis=0, axis_index_groups=sides, tiled=True)
+    recv = lax.all_to_all(
+        decoded, "replica", split_axis=0, concat_axis=0, axis_index_groups=first_sides, tiled=True
+    )
     mine = pl.pallas_call(
         chip_sum_kernel,
         compiler_params=PARAMS,

time: 40.8 us -> 39.8 us (0.975)
  blocking collectives: 37.3 us -> 36.6 us
    all_gather x1, blocking collectives: 8.66 us -> 6.95 us  [per_device(): lax.all_gather(mine, 'replica', axis=0, axis_index_groups=pairs, tiled=True)]
    all_to_all x1, blocking collectives: 18.3 us -> 19.4 us  [per_device(): lax.all_to_all(decoded, 'replica', split_axis=0, concat_axis=0, axis_inde...]
where the time goes in v5:
time: 39.8 us; the launch traced here: 39.4 us
  blocking collectives  36.6 us (92%)
  Pallas kernels  2.08 us (5%)
  between operations  0.71 us (2%)
    all_to_all x1, blocking collectives, per_device(): lax.all_to_all(decoded, 'replica', split_axis=0, concat_axis=0, axis_inde...  19.4 us
    all_to_all x1, blocking collectives, per_device(): lax.all_to_all(shared, 'replica', split_axis=0, concat_axis=0, axis_index...  10.2 us
    all_gather x1, blocking collectives, per_device(): lax.all_gather(mine, 'replica', axis=0, axis_index_groups=pairs, tiled=True)  6.95 us
    pallas_call x1, Pallas kernels, per_device(): pl.pallas_call(decode_kernel, compiler_params=PARAMS, out_shape=chunks, i...  1.25 us

profile of v5, /device:TPU:1, one launch (start us, length us, event | category | flops | bytes accessed | tf_op | source)
XLA Modules:
  0.0 39.4 jit_solution(7656511583097140635)
XLA Ops:
  0.6 1.2 %shard_map.154 = bf16[32,16,128]{2,1,0:T(8,128)(2,1)S(1)} custom-call(s32[16]{0:T(128)} %table_hbm.1, s32[2,32,896]{2,1,0:T(8,128)} %bitcast.14, s32[7,2,32]{2,1,0:T(2,128)} %bitcast.16, s32[32,256]{1,0:T(8,128)} %bitcast.15, s32[2,32]{1,0:T(2,128)} %bitcast.17), custom_call_target="tpu_custom_call" | custom-call | tf_op jit(solution)/shard_map/pallas_call | solution.py:156
  1.9 0.0 copy-start.2
  1.9 0.0 copy-start.3
  1.9 0.0 copy-start.4
  1.9 0.0 copy-start.5
  1.9 19.4 %all_to_all.10.recv = bf16[32,16,128]{2,1,0:T(8,128)(2,1)S(1)} all-to-all(bf16[32,16,128]{2,1,0:T(8,128)(2,1)S(1)} %shard_map.154), channel_id=1, replica_groups={{32,64,128,192,256,320,384,448,512,576,640,704,768,832,896,960},{0,96,1..., dimensions={0} | all-to-all | bytes 262144 | tf_op jit(solution)/shard_map/all_to_all | solution.py:173
  21.4 0.0 copy-done.2
  21.4 0.0 copy-done.3
  21.4 0.0 copy-done.4
  21.4 0.0 copy-done.5
  21.4 6.9 %all_gather.3.both = f32[8,16,128]{2,1,0:T(8,128)S(1)} all-gather(f32[4,16,128]{2,1,0:T(8,128)S(1)} %shard_map.155), channel_id=1, replica_groups={{0,32},{64,96},{128,160},{192,224},{256,288},{320,352},{384,416},{448,4..., dimensions={0}, use_global_device_ids=true | all-gather | bytes 98304 | tf_op jit(solution)/shard_map/all_gather | solution.py:183
  28.4 0.0 copy-start
  28.4 0.0 copy-start.1
  28.4 10.2 %all_to_all.11.recv = bf16[32,16,128]{2,1,0:T(8,128)(2,1)S(1)} all-to-all(bf16[32,16,128]{2,1,0:T(8,128)(2,1)S(1)} %get-tuple-element.14), channel_id=1, replica_groups={{0,64,128,192,256,320,384,448,512,576,640,704,768,832,896,960},{32,96,1..., dimensions={0} | all-to-all | bytes 262144 | tf_op jit(solution)/shard_map/all_to_all | solution.py:192
  38.6 0.0 copy-done
  38.6 0.0 copy-done.1
  38.6 0.8 %shard_map.157 = (bf16[2,32,896]{2,1,0:T(8,128)(2,1)}, bf16[32,256]{1,0:T(8,128)(2,1)}, f32[2,1,896]{2,1,0:T(1,128)}, f32[2,1,896]{2,1,0:T(1,128)}, f32[1,256]{1,0:T(1,128)}, /*index=5*/f32[1,256]{1,0:T(1,128)}) custom-call(bf16[32,16,128]{2,1,0:T(8,128)(2,1)S(1)} %all_to_all.11.recv, bf16[2,32,896]{2,1,0:T(8,128)(2,1)S(1)} %bitcast.12, ...), custom_call_target="tpu_custom_call" | custom-call | tf_op jit(solution)/shard_map/pallas_call | solution.py:193
  (2 shorter events, 0.0 us)
Async XLA Ops:
  1.9 19.5 %copy-start.2 = (f32[2,1,896]{2,1,0:T(1,128)S(1)}, f32[2,1,896]{2,1,0:T(1,128)}, u32[]{:S(2)}) copy-start(f32[2,1,896]{2,1,0:T(1,128)} %up_global.1) | copy-start | bytes 21508
  1.9 19.5 %copy-start.3 = (f32[2,1,896]{2,1,0:T(1,128)S(1)}, f32[2,1,896]{2,1,0:T(1,128)}, u32[]{:S(2)}) copy-start(f32[2,1,896]{2,1,0:T(1,128)} %up_moment.1) | copy-start | bytes 21508
  1.9 19.5 %copy-start.4 = (f32[1,256]{1,0:T(1,128)S(1)}, f32[1,256]{1,0:T(1,128)}, u32[]{:S(2)}) copy-start(f32[1,256]{1,0:T(1,128)} %down_global.1) | copy-start | bytes 3076
  1.9 19.4 %copy-start.5 = (f32[1,256]{1,0:T(1,128)S(1)}, f32[1,256]{1,0:T(1,128)}, u32[]{:S(2)}) copy-start(f32[1,256]{1,0:T(1,128)} %down_moment.1) | copy-start | bytes 3076
  28.4 10.3 %copy-start = (bf16[1,2,32,896]{3,2,1,0:T(8,128)(2,1)S(1)}, bf16[1,2,32,896]{3,2,1,0:T(8,128)(2,1)}, u32[]{:S(2)}) copy-start(bf16[1,2,32,896]{3,2,1,0:T(8,128)(2,1)} %param.16) | copy-start | bytes 344068
  28.4 10.2 %copy-start.1 = (bf16[1,32,256]{2,1,0:T(8,128)(2,1)S(1)}, bf16[1,32,256]{2,1,0:T(8,128)(2,1)}, u32[]{:S(2)}) copy-start(bf16[1,32,256]{2,1,0:T(8,128)(2,1)} %param.21) | copy-start | bytes 49156

commit v6 on v5

--- a/solution.py
+++ b/solution.py
@@ -148,6 +148,7 @@
     pairs = [[2 * q, 2 * q + 1] for q in range(chips)]
     sides = [[2 * q + c for q in range(chips)] for c in range(2)]
     first_sides = [[1 - c] + side[1:] for c, side in enumerate(sides)]
+    second_sides = [side[:1] + sides[1 - c][1:4] + side[4:] for c, side in enumerate(sides)]
     sds = jax.ShapeDtypeStruct
     chunks = sds((rows, slots, LANES), jnp.bfloat16)
     up_exps = jnp.transpose(up_exps[0], (2, 0, 1))
@@ -189,7 +190,9 @@
         out_specs=(VMEM,) * 2,
         scratch_shapes=[pltpu.VMEM((2, 2, slots, LANES), jnp.float32)],
     )(both)
-    spread = lax.all_to_all(shared, "replica", split_axis=0, concat_axis=0, axis_index_groups=sides, tiled=True)
+    spread = lax.all_to_all(
+        shared, "replica", split_axis=0, concat_axis=0, axis_index_groups=second_sides, tiled=True
+    )
     up_merged, down_merged, up_new, up_mom, down_new, down_mom = pl.pallas_call(
         merge_kernel,
         compiler_params=PARAMS,

time: 39.8 us -> 39.8 us (level)
  no operation moved by 1% of the time
where the time goes in v6:
time: 39.8 us; the launch traced here: 39.4 us
  blocking collectives  36.6 us (92%)
  Pallas kernels  2.08 us (5%)
  between operations  0.71 us (2%)
    all_to_all x1, blocking collectives, per_device(): lax.all_to_all(decoded, 'replica', split_axis=0, concat_axis=0, axis_inde...  19.4 us
    all_to_all x1, blocking collectives, per_device(): lax.all_to_all(shared, 'replica', split_axis=0, concat_axis=0, axis_index...  10.2 us
    all_gather x1, blocking collectives, per_device(): lax.all_gather(mine, 'replica', axis=0, axis_index_groups=pairs, tiled=True)  6.95 us
    pallas_call x1, Pallas kernels, per_device(): pl.pallas_call(decode_kernel, compiler_params=PARAMS, out_shape=chunks, i...  1.25 us

profile of v6, /device:TPU:1, one launch (start us, length us, event | category | flops | bytes accessed | tf_op | source)
XLA Modules:
  0.0 39.4 jit_solution(9906232374279601128)
XLA Ops:
  0.6 1.2 %shard_map.154 = bf16[32,16,128]{2,1,0:T(8,128)(2,1)S(1)} custom-call(s32[16]{0:T(128)} %table_hbm.1, s32[2,32,896]{2,1,0:T(8,128)} %bitcast.14, s32[7,2,32]{2,1,0:T(2,128)} %bitcast.16, s32[32,256]{1,0:T(8,128)} %bitcast.15, s32[2,32]{1,0:T(2,128)} %bitcast.17), custom_call_target="tpu_custom_call" | custom-call | tf_op jit(solution)/shard_map/pallas_call | solution.py:157
  1.9 0.0 copy-start.2
  1.9 0.0 copy-start.3
  1.9 0.0 copy-start.4
  1.9 0.0 copy-start.5
  1.9 19.4 %all_to_all.10.recv = bf16[32,16,128]{2,1,0:T(8,128)(2,1)S(1)} all-to-all(bf16[32,16,128]{2,1,0:T(8,128)(2,1)S(1)} %shard_map.154), channel_id=1, replica_groups={{32,64,128,192,256,320,384,448,512,576,640,704,768,832,896,960},{0,96,1..., dimensions={0} | all-to-all | bytes 262144 | tf_op jit(solution)/shard_map/all_to_all | solution.py:174
  21.4 0.0 copy-done.2
  21.4 0.0 copy-done.3
  21.4 0.0 copy-done.4
  21.4 0.0 copy-done.5
  21.4 6.9 %all_gather.3.both = f32[8,16,128]{2,1,0:T(8,128)S(1)} all-gather(f32[4,16,128]{2,1,0:T(8,128)S(1)} %shard_map.155), channel_id=1, replica_groups={{0,32},{64,96},{128,160},{192,224},{256,288},{320,352},{384,416},{448,4..., dimensions={0}, use_global_device_ids=true | all-gather | bytes 98304 | tf_op jit(solution)/shard_map/all_gather | solution.py:184
  28.4 0.0 copy-start
  28.4 0.0 copy-start.1
  28.4 10.2 %all_to_all.11.recv = bf16[32,16,128]{2,1,0:T(8,128)(2,1)S(1)} all-to-all(bf16[32,16,128]{2,1,0:T(8,128)(2,1)S(1)} %get-tuple-element.14), channel_id=1, replica_groups={{0,96,160,224,256,320,384,448,512,576,640,704,768,832,896,960},{32,64,1..., dimensions={0} | all-to-all | bytes 262144 | tf_op jit(solution)/shard_map/all_to_all | solution.py:193
  38.6 0.0 copy-done
  38.6 0.0 copy-done.1
  38.6 0.8 %shard_map.157 = (bf16[2,32,896]{2,1,0:T(8,128)(2,1)}, bf16[32,256]{1,0:T(8,128)(2,1)}, f32[2,1,896]{2,1,0:T(1,128)}, f32[2,1,896]{2,1,0:T(1,128)}, f32[1,256]{1,0:T(1,128)}, /*index=5*/f32[1,256]{1,0:T(1,128)}) custom-call(bf16[32,16,128]{2,1,0:T(8,128)(2,1)S(1)} %all_to_all.11.recv, bf16[2,32,896]{2,1,0:T(8,128)(2,1)S(1)} %bitcast.12, ...), custom_call_target="tpu_custom_call" | custom-call | tf_op jit(solution)/shard_map/pallas_call | solution.py:196
  (2 shorter events, 0.0 us)
Async XLA Ops:
  1.9 19.5 %copy-start.2 = (f32[2,1,896]{2,1,0:T(1,128)S(1)}, f32[2,1,896]{2,1,0:T(1,128)}, u32[]{:S(2)}) copy-start(f32[2,1,896]{2,1,0:T(1,128)} %up_global.1) | copy-start | bytes 21508
  1.9 19.5 %copy-start.3 = (f32[2,1,896]{2,1,0:T(1,128)S(1)}, f32[2,1,896]{2,1,0:T(1,128)}, u32[]{:S(2)}) copy-start(f32[2,1,896]{2,1,0:T(1,128)} %up_moment.1) | copy-start | bytes 21508
  1.9 19.5 %copy-start.4 = (f32[1,256]{1,0:T(1,128)S(1)}, f32[1,256]{1,0:T(1,128)}, u32[]{:S(2)}) copy-start(f32[1,256]{1,0:T(1,128)} %down_global.1) | copy-start | bytes 3076
  1.9 19.4 %copy-start.5 = (f32[1,256]{1,0:T(1,128)S(1)}, f32[1,256]{1,0:T(1,128)}, u32[]{:S(2)}) copy-start(f32[1,256]{1,0:T(1,128)} %down_moment.1) | copy-start | bytes 3076
  28.4 10.3 %copy-start = (bf16[1,2,32,896]{3,2,1,0:T(8,128)(2,1)S(1)}, bf16[1,2,32,896]{3,2,1,0:T(8,128)(2,1)}, u32[]{:S(2)}) copy-start(bf16[1,2,32,896]{3,2,1,0:T(8,128)(2,1)} %param.16) | copy-start | bytes 344068
  28.4 10.2 %copy-start.1 = (bf16[1,32,256]{2,1,0:T(8,128)(2,1)S(1)}, bf16[1,32,256]{2,1,0:T(8,128)(2,1)}, u32[]{:S(2)}) copy-start(bf16[1,32,256]{2,1,0:T(8,128)(2,1)} %param.21) | copy-start | bytes 49156

commit v7 on v6

--- a/solution.py
+++ b/solution.py
@@ -66,7 +66,7 @@
             odd = (codes & (1 << bit)) != 0
             values = [jnp.where(odd, values[i + 1], values[i]) for i in range(0, len(values), 2)]
         values = values[0]
-        out_ref[r] = (values * scales[:, r : r + 1]).astype(jnp.bfloat16)
+        out_ref[(r + rows // 2) % rows] = (values * scales[:, r : r + 1]).astype(jnp.bfloat16)
 
 
 def chip_sum_kernel(recv, up_global, up_moment, down_global, down_moment, out_ref):
@@ -109,7 +109,7 @@
     down_blocks = down_local.shape[1] // LANES
     slots = recv.shape[1]
     for r in range(rows):
-        shared[r * slots : (r + 1) * slots, :] = recv[r].astype(jnp.float32)
+        shared[r * slots : (r + 1) * slots, :] = recv[(r + rows // 2) % rows].astype(jnp.float32)
 
     def merged(local, j):
         theirs = shared[pl.ds(j, rows, stride=slots), :]
@@ -146,9 +146,9 @@
     slots = (groups * width + depth) // LANES
     chips = rows // 2
     pairs = [[2 * q, 2 * q + 1] for q in range(chips)]
-    sides = [[2 * q + c for q in range(chips)] for c in range(2)]
-    first_sides = [[1 - c] + side[1:] for c, side in enumerate(sides)]
-    second_sides = [side[:1] + sides[1 - c][1:4] + side[4:] for c, side in enumerate(sides)]
+    order = [(q + chips // 2) % chips for q in range(chips)]
+    first_sides = [[2 * q + (c if q else 1 - c) for q in order] for c in range(2)]
+    second_sides = [[2 * q + c for q in order] for c in range(2)]
     sds = jax.ShapeDtypeStruct
     chunks = sds((rows, slots, LANES), jnp.bfloat16)
     up_exps = jnp.transpose(up_exps[0], (2, 0, 1))

time: 39.8 us -> 38.9 us (0.977)
  blocking collectives: 36.6 us -> 35.6 us
    all_gather x1, blocking collectives: 6.95 us -> 6.39 us  [per_device(): lax.all_gather(mine, 'replica', axis=0, axis_index_groups=pairs, tiled=True)]
where the time goes in v7:
time: 38.9 us; the launch traced here: 38.4 us
  blocking collectives  35.6 us (92%)
  Pallas kernels  2.08 us (5%)
  between operations  0.71 us (2%)
    all_to_all x1, blocking collectives, per_device(): lax.all_to_all(decoded, 'replica', split_axis=0, concat_axis=0, axis_inde...  19.2 us
    all_to_all x1, blocking collectives, per_device(): lax.all_to_all(shared, 'replica', split_axis=0, concat_axis=0, axis_index...  9.99 us
    all_gather x1, blocking collectives, per_device(): lax.all_gather(mine, 'replica', axis=0, axis_index_groups=pairs, tiled=True)  6.39 us
    pallas_call x1, Pallas kernels, per_device(): pl.pallas_call(decode_kernel, compiler_params=PARAMS, out_shape=chunks, i...  1.25 us
    pallas_call x1, Pallas kernels, per_device(): pl.pallas_call(merge_kernel, compiler_params=PARAMS, out_shape=(sds(up_lo...  0.79 us

profile of v7, /device:TPU:1, one launch (start us, length us, event | category | flops | bytes accessed | tf_op | source)
XLA Modules:
  0.0 38.4 jit_solution(6289686696113147503)
XLA Ops:
  0.6 1.2 %shard_map.154 = bf16[32,16,128]{2,1,0:T(8,128)(2,1)S(1)} custom-call(s32[16]{0:T(128)} %table_hbm.1, s32[2,32,896]{2,1,0:T(8,128)} %bitcast.14, s32[7,2,32]{2,1,0:T(2,128)} %bitcast.16, s32[32,256]{1,0:T(8,128)} %bitcast.15, s32[2,32]{1,0:T(2,128)} %bitcast.17), custom_call_target="tpu_custom_call" | custom-call | tf_op jit(solution)/shard_map/pallas_call | solution.py:157
  1.9 0.0 copy-start.2
  1.9 0.0 copy-start.3
  1.9 0.0 copy-start.4
  1.9 0.0 copy-start.5
  1.9 19.2 %all_to_all.10.recv = bf16[32,16,128]{2,1,0:T(8,128)(2,1)S(1)} all-to-all(bf16[32,16,128]{2,1,0:T(8,128)(2,1)S(1)} %shard_map.154), channel_id=1, replica_groups={{512,576,640,704,768,832,896,960,32,64,128,192,256,320,384,448},{544,60..., dimensions={0} | all-to-all | bytes 262144 | tf_op jit(solution)/shard_map/all_to_all | solution.py:174
  21.1 0.0 copy-done.2
  21.2 0.0 copy-done.3
  21.2 0.0 copy-done.4
  21.2 0.0 copy-done.5
  21.2 6.4 %all_gather.3.both = f32[8,16,128]{2,1,0:T(8,128)S(1)} all-gather(f32[4,16,128]{2,1,0:T(8,128)S(1)} %shard_map.155), channel_id=1, replica_groups={{0,32},{64,96},{128,160},{192,224},{256,288},{320,352},{384,416},{448,4..., dimensions={0}, use_global_device_ids=true | all-gather | bytes 98304 | tf_op jit(solution)/shard_map/all_gather | solution.py:184
  27.6 0.0 copy-start
  27.6 0.0 copy-start.1
  27.6 10.0 %all_to_all.11.recv = bf16[32,16,128]{2,1,0:T(8,128)(2,1)S(1)} all-to-all(bf16[32,16,128]{2,1,0:T(8,128)(2,1)S(1)} %get-tuple-element.14), channel_id=1, replica_groups={{512,576,640,704,768,832,896,960,0,64,128,192,256,320,384,448},{544,608..., dimensions={0} | all-to-all | bytes 262144 | tf_op jit(solution)/shard_map/all_to_all | solution.py:193
  37.6 0.0 copy-done
  37.6 0.0 copy-done.1
  37.6 0.8 %shard_map.157 = (bf16[2,32,896]{2,1,0:T(8,128)(2,1)}, bf16[32,256]{1,0:T(8,128)(2,1)}, f32[2,1,896]{2,1,0:T(1,128)}, f32[2,1,896]{2,1,0:T(1,128)}, f32[1,256]{1,0:T(1,128)}, /*index=5*/f32[1,256]{1,0:T(1,128)}) custom-call(bf16[32,16,128]{2,1,0:T(8,128)(2,1)S(1)} %all_to_all.11.recv, bf16[2,32,896]{2,1,0:T(8,128)(2,1)S(1)} %bitcast.12, ...), custom_call_target="tpu_custom_call" | custom-call | tf_op jit(solution)/shard_map/pallas_call | solution.py:196
  (2 shorter events, 0.0 us)
Async XLA Ops:
  1.9 19.3 %copy-start.2 = (f32[2,1,896]{2,1,0:T(1,128)S(1)}, f32[2,1,896]{2,1,0:T(1,128)}, u32[]{:S(2)}) copy-start(f32[2,1,896]{2,1,0:T(1,128)} %up_global.1) | copy-start | bytes 21508
  1.9 19.3 %copy-start.3 = (f32[2,1,896]{2,1,0:T(1,128)S(1)}, f32[2,1,896]{2,1,0:T(1,128)}, u32[]{:S(2)}) copy-start(f32[2,1,896]{2,1,0:T(1,128)} %up_moment.1) | copy-start | bytes 21508
  1.9 19.2 %copy-start.4 = (f32[1,256]{1,0:T(1,128)S(1)}, f32[1,256]{1,0:T(1,128)}, u32[]{:S(2)}) copy-start(f32[1,256]{1,0:T(1,128)} %down_global.1) | copy-start | bytes 3076
  1.9 19.2 %copy-start.5 = (f32[1,256]{1,0:T(1,128)S(1)}, f32[1,256]{1,0:T(1,128)}, u32[]{:S(2)}) copy-start(f32[1,256]{1,0:T(1,128)} %down_moment.1) | copy-start | bytes 3076
  27.6 10.0 %copy-start = (bf16[1,2,32,896]{3,2,1,0:T(8,128)(2,1)S(1)}, bf16[1,2,32,896]{3,2,1,0:T(8,128)(2,1)}, u32[]{:S(2)}) copy-start(bf16[1,2,32,896]{3,2,1,0:T(8,128)(2,1)} %param.16) | copy-start | bytes 344068
  27.6 10.0 %copy-start.1 = (bf16[1,32,256]{2,1,0:T(8,128)(2,1)S(1)}, bf16[1,32,256]{2,1,0:T(8,128)(2,1)}, u32[]{:S(2)}) copy-start(bf16[1,32,256]{2,1,0:T(8,128)(2,1)} %param.21) | copy-start | bytes 49156

commit v8 on v7

--- a/solution.py
+++ b/solution.py
@@ -25,7 +25,7 @@
 
 def decode_kernel(
     table_hbm, up_codes_hbm, up_exps_hbm, down_codes_hbm, down_exps_hbm, out_ref,
-    table_ref, up_codes, up_exps, down_codes, down_exps, codes_by_row, exps_by_slot, sems,
+    table_ref, up_codes, up_exps, down_codes, down_exps, values_by_row, exps_by_slot, sems,
 ):
     copies = [
         pltpu.make_async_copy(source, target, sems.at[i])
@@ -47,25 +47,28 @@
     slots = groups * up_blocks + down_blocks
     copies[0].wait()
     table = [table_ref[level].astype(jnp.float32) for level in range(16)]
-    for copy in copies[1:4]:
-        copy.wait()
-    for j, g, s in up_slots(groups, up_blocks):
-        exps_by_slot[j : j + 1, :] = up_exps[s, g : g + 1, :]
-    for t in range(down_blocks):
-        j = groups * up_blocks + t
-        codes_by_row[pl.ds(j, rows, stride=slots), :] = down_codes[:, t * LANES : (t + 1) * LANES]
-        exps_by_slot[j : j + 1, :] = down_exps[t : t + 1, :]
-    scales = jnp.left_shift(1, exps_by_slot[...] - LOW_EXP).astype(jnp.float32) * 2.0**LOW_EXP
-    copies[4].wait()
-    for j, g, s in up_slots(groups, up_blocks):
-        codes_by_row[pl.ds(j, rows, stride=slots), :] = up_codes[g, :, s * LANES : (s + 1) * LANES]
-    for r in range(rows):
-        codes = codes_by_row[r * slots : (r + 1) * slots, :]
+    def look_up(codes):
         values = table
         for bit in range(4):
             odd = (codes & (1 << bit)) != 0
             values = [jnp.where(odd, values[i + 1], values[i]) for i in range(0, len(values), 2)]
-        values = values[0]
+        return values[0]
+
+    for copy in copies[1:4]:
+        copy.wait()
+    for j, g, s in up_slots(groups, up_blocks):
+        exps_by_slot[j : j + 1, :] = up_exps[s, g : g + 1, :]
+    for t in range(down_blocks):
+        j = groups * up_blocks + t
+        values_by_row[pl.ds(j, rows, stride=slots), :] = look_up(down_codes[:, t * LANES : (t + 1) * LANES])
+        exps_by_slot[j : j + 1, :] = down_exps[t : t + 1, :]
+    scales = jnp.left_shift(1, exps_by_slot[...] - LOW_EXP).astype(jnp.float32) * 2.0**LOW_EXP
+    copies[4].wait()
+    for j, g, s in up_slots(groups, up_blocks):
+        block = up_codes[g, :, s * LANES : (s + 1) * LANES]
+        values_by_row[pl.ds(j, rows, stride=slots), :] = look_up(block)
+    for r in range(rows):
+        values = values_by_row[r * slots : (r + 1) * slots, :]
         out_ref[(r + rows // 2) % rows] = (values * scales[:, r : r + 1]).astype(jnp.bfloat16)
 
 
@@ -166,7 +169,7 @@
             pltpu.VMEM(up_exps.shape, jnp.int32),
             pltpu.VMEM(down_codes.shape[1:], jnp.int32),
             pltpu.VMEM(down_exps.shape, jnp.int32),
-            pltpu.VMEM((rows * slots, LANES), jnp.int32),
+            pltpu.VMEM((rows * slots, LANES), jnp.float32),
             pltpu.VMEM((slots, rows), jnp.int32),
             pltpu.SemaphoreType.DMA((5,)),
         ],

time: 38.9 us -> 38.9 us (level)
  no operation moved by 1% of the time
where the time goes in v8:
time: 38.9 us; the launch traced here: 38.4 us
  blocking collectives  35.6 us (92%)
  Pallas kernels  2.03 us (5%)
  between operations  0.71 us (2%)
    all_to_all x1, blocking collectives, per_device(): lax.all_to_all(decoded, 'replica', split_axis=0, concat_axis=0, axis_inde...  19.2 us
    all_to_all x1, blocking collectives, per_device(): lax.all_to_all(shared, 'replica', split_axis=0, concat_axis=0, axis_index...  9.99 us
    all_gather x1, blocking collectives, per_device(): lax.all_gather(mine, 'replica', axis=0, axis_index_groups=pairs, tiled=True)  6.39 us
    pallas_call x1, Pallas kernels, per_device(): pl.pallas_call(decode_kernel, compiler_params=PARAMS, out_shape=chunks, i...  1.2 us
    pallas_call x1, Pallas kernels, per_device(): pl.pallas_call(merge_kernel, compiler_params=PARAMS, out_shape=(sds(up_lo...  0.79 us

profile of v8, /device:TPU:1, one launch (start us, length us, event | category | flops | bytes accessed | tf_op | source)
XLA Modules:
  0.0 38.4 jit_solution(2728920231278468802)
XLA Ops:
  0.6 1.2 %shard_map.154 = bf16[32,16,128]{2,1,0:T(8,128)(2,1)S(1)} custom-call(s32[16]{0:T(128)} %table_hbm.1, s32[2,32,896]{2,1,0:T(8,128)} %bitcast.14, s32[7,2,32]{2,1,0:T(2,128)} %bitcast.16, s32[32,256]{1,0:T(8,128)} %bitcast.15, s32[2,32]{1,0:T(2,128)} %bitcast.17), custom_call_target="tpu_custom_call" | custom-call | tf_op jit(solution)/shard_map/pallas_call | solution.py:160
  1.8 0.0 copy-start.2
  1.8 0.0 copy-start.3
  1.9 0.0 copy-start.4
  1.9 0.0 copy-start.5
  1.9 19.2 %all_to_all.10.recv = bf16[32,16,128]{2,1,0:T(8,128)(2,1)S(1)} all-to-all(bf16[32,16,128]{2,1,0:T(8,128)(2,1)S(1)} %shard_map.154), channel_id=1, replica_groups={{512,576,640,704,768,832,896,960,32,64,128,192,256,320,384,448},{544,60..., dimensions={0} | all-to-all | bytes 262144 | tf_op jit(solution)/shard_map/all_to_all | solution.py:177
  21.1 0.0 copy-done.2
  21.1 0.0 copy-done.3
  21.1 0.0 copy-done.4
  21.1 0.0 copy-done.5
  21.1 6.4 %all_gather.3.both = f32[8,16,128]{2,1,0:T(8,128)S(1)} all-gather(f32[4,16,128]{2,1,0:T(8,128)S(1)} %shard_map.155), channel_id=1, replica_groups={{0,32},{64,96},{128,160},{192,224},{256,288},{320,352},{384,416},{448,4..., dimensions={0}, use_global_device_ids=true | all-gather | bytes 98304 | tf_op jit(solution)/shard_map/all_gather | solution.py:187
  27.6 0.0 copy-start
  27.6 0.0 copy-start.1
  27.6 10.0 %all_to_all.11.recv = bf16[32,16,128]{2,1,0:T(8,128)(2,1)S(1)} all-to-all(bf16[32,16,128]{2,1,0:T(8,128)(2,1)S(1)} %get-tuple-element.14), channel_id=1, replica_groups={{512,576,640,704,768,832,896,960,0,64,128,192,256,320,384,448},{544,608..., dimensions={0} | all-to-all | bytes 262144 | tf_op jit(solution)/shard_map/all_to_all | solution.py:196
  37.6 0.0 copy-done
  37.6 0.0 copy-done.1
  37.6 0.8 %shard_map.157 = (bf16[2,32,896]{2,1,0:T(8,128)(2,1)}, bf16[32,256]{1,0:T(8,128)(2,1)}, f32[2,1,896]{2,1,0:T(1,128)}, f32[2,1,896]{2,1,0:T(1,128)}, f32[1,256]{1,0:T(1,128)}, /*index=5*/f32[1,256]{1,0:T(1,128)}) custom-call(bf16[32,16,128]{2,1,0:T(8,128)(2,1)S(1)} %all_to_all.11.recv, bf16[2,32,896]{2,1,0:T(8,128)(2,1)S(1)} %bitcast.12, ...), custom_call_target="tpu_custom_call" | custom-call | tf_op jit(solution)/shard_map/pallas_call | solution.py:199
  (2 shorter events, 0.0 us)
Async XLA Ops:
  1.8 19.3 %copy-start.2 = (f32[2,1,896]{2,1,0:T(1,128)S(1)}, f32[2,1,896]{2,1,0:T(1,128)}, u32[]{:S(2)}) copy-start(f32[2,1,896]{2,1,0:T(1,128)} %up_global.1) | copy-start | bytes 21508
  1.8 19.3 %copy-start.3 = (f32[2,1,896]{2,1,0:T(1,128)S(1)}, f32[2,1,896]{2,1,0:T(1,128)}, u32[]{:S(2)}) copy-start(f32[2,1,896]{2,1,0:T(1,128)} %up_moment.1) | copy-start | bytes 21508
  1.9 19.2 %copy-start.4 = (f32[1,256]{1,0:T(1,128)S(1)}, f32[1,256]{1,0:T(1,128)}, u32[]{:S(2)}) copy-start(f32[1,256]{1,0:T(1,128)} %down_global.1) | copy-start | bytes 3076
  1.9 19.2 %copy-start.5 = (f32[1,256]{1,0:T(1,128)S(1)}, f32[1,256]{1,0:T(1,128)}, u32[]{:S(2)}) copy-start(f32[1,256]{1,0:T(1,128)} %down_moment.1) | copy-start | bytes 3076
  27.6 10.0 %copy-start = (bf16[1,2,32,896]{3,2,1,0:T(8,128)(2,1)S(1)}, bf16[1,2,32,896]{3,2,1,0:T(8,128)(2,1)}, u32[]{:S(2)}) copy-start(bf16[1,2,32,896]{3,2,1,0:T(8,128)(2,1)} %param.16) | copy-start | bytes 344068
  27.6 10.0 %copy-start.1 = (bf16[1,32,256]{2,1,0:T(8,128)(2,1)S(1)}, bf16[1,32,256]{2,1,0:T(8,128)(2,1)}, u32[]{:S(2)}) copy-start(bf16[1,32,256]{2,1,0:T(8,128)(2,1)} %param.21) | copy-start | bytes 49156
